TPU v7x, 32 devices: a whole 2x2x4 slice. The times are simulated.
32 devices in a mesh: section: 2 (over y), fsdp: 16 (over z, x, core).
Axes of the slice: x: 2, y: 2, z: 4, core: 2. Of those that a mesh axis runs over, the one named last changes fastest.
Arguments:
- images: bfloat16 [64, 197, 768], P('fsdp'), may hold values from -6 to 6
- cotangent: bfloat16 [64, 197, 768], P('fsdp'), may hold values from -6 to 6
- live_slots: int32 [64], P('fsdp'), may hold values from 0 to 1, as said below
- normgain: bfloat16 [2, 768], P('section', 'fsdp'), may hold values from 0.099609375 to 1.8984375
- normbias: bfloat16 [2, 768], P('section', 'fsdp'), may hold values from -3 to 3
- qkvweight: bfloat16 [2, 768, 2304], P('section', 'fsdp'), may hold values from -0.21875 to 0.21875
- qvbias: bfloat16 [2, 1536], P('section', 'fsdp'), may hold values from -3 to 3
- outweight: bfloat16 [2, 768, 768], P('section', 'fsdp'), may hold values from -1.75 to 1.75
- outbias: bfloat16 [2, 768], P('section', 'fsdp'), may hold values from -3 to 3
- mlpgain: bfloat16 [2, 768], P('section', 'fsdp'), may hold values from 0.099609375 to 1.8984375
- mlpbias: bfloat16 [2, 768], P('section', 'fsdp'), may hold values from -3 to 3
- upweight: bfloat16 [2, 768, 3072], P('section', 'fsdp'), may hold values from -0.21875 to 0.21875
- upbias: bfloat16 [2, 3072], P('section', 'fsdp'), may hold values from -3 to 3
- downweight: bfloat16 [2, 3072, 768], P('section', 'fsdp'), may hold values from -0.109375 to 0.109375
- downbias: bfloat16 [2, 768], P('section', 'fsdp'), may hold values from -3 to 3
Outputs:
- exits: bfloat16 [2, 64, 197, 768], P('section', 'fsdp')
- entry_grads: bfloat16 [2, 64, 197, 768], P('section', 'fsdp')
- normgain_grad: float32 [2, 768], P('section', 'fsdp')
- normbias_grad: float32 [2, 768], P('section', 'fsdp')
- qkvweight_grad: float32 [2, 768, 2304], P('section', 'fsdp')
- qvbias_grad: float32 [2, 1536], P('section', 'fsdp')
- outweight_grad: float32 [2, 768, 768], P('section', 'fsdp')
- outbias_grad: float32 [2, 768], P('section', 'fsdp')
- mlpgain_grad: float32 [2, 768], P('section', 'fsdp')
- mlpbias_grad: float32 [2, 768], P('section', 'fsdp')
- upweight_grad: float32 [2, 768, 3072], P('section', 'fsdp')
- upbias_grad: float32 [2, 3072], P('section', 'fsdp')
- downweight_grad: float32 [2, 3072, 768], P('section', 'fsdp')
- downbias_grad: float32 [2, 768], P('section', 'fsdp')
Inputs may be any that keep to these rules, and one draw needn't show every extreme that they name: `live_slots`: exactly 49 of the 64 slots hold an image (1); the rest are empty (0).
All inputs are finite; a program needn't handle non-finite values.
Results may differ from a plain program's by a relative error of at most 0.014.
Values may be sent and summed in bfloat16 or wider, within the bound.
A program may use at most 256 MiB of HBM per device.

v0:
```python
from functools import partial

import jax
import jax.numpy as jnp
from jax import lax
from jax.sharding import PartitionSpec as P

HEADS = 12
HEAD = 64
MB = 4


EPSILON = 1e-06


def from_behind(value, axis, by):
    peers = lax.axis_size(axis)
    pairs = [(i, i + by) for i in range(peers) if 0 <= i + by < peers]
    return lax.ppermute(value, axis, pairs)


def layer_norm(row_data, gain_row, shift_row):
    center = row_data - jnp.mean(row_data, axis=-1, keepdims=True)
    spread = jnp.mean(center * center, axis=-1, keepdims=True)
    return center * lax.rsqrt(spread + EPSILON) * gain_row + shift_row


def softmax_rows(scores):
    top_score = jnp.max(scores, axis=-1, keepdims=True)
    expo = jnp.exp(scores - top_score)
    return expo / jnp.sum(expo, axis=-1, keepdims=True)


def block_forward(weights, row_data, count_images):
    (
        normgain,
        normbias,
        qkvweight,
        qvbias,
        outweight,
        outbias,
        mlpgain,
        mlpbias,
        upweight,
        upbias,
        downweight,
        downbias,
    ) = weights
    row_count, model_width = row_data.shape
    qscale = HEAD ** (-0.5)
    row_float = row_data.astype(jnp.float32)
    normed = layer_norm(
        row_float, normgain.astype(jnp.float32), normbias.astype(jnp.float32)
    ).astype(jnp.bfloat16)
    joint = jnp.dot(normed, qkvweight, preferred_element_type=jnp.float32)
    bias_float = qvbias.astype(jnp.float32)
    queries = ((joint[:, :model_width] + bias_float[:model_width]) * qscale).astype(jnp.bfloat16)
    keys_all = joint[:, model_width : 2 * model_width].astype(jnp.bfloat16)
    values = (joint[:, 2 * model_width :] + bias_float[model_width:]).astype(jnp.bfloat16)
    head_shape = (count_images, row_count // count_images, HEADS, HEAD)
    head_q = queries.reshape(head_shape)
    head_k = keys_all.reshape(head_shape)
    head_v = values.reshape(head_shape)
    scores = jnp.einsum("iqhd,ikhd->ihqk", head_q, head_k, preferred_element_type=jnp.float32)
    attn_low = softmax_rows(scores).astype(jnp.bfloat16)
    mixed = jnp.einsum("ihqk,ikhd->iqhd", attn_low, head_v, preferred_element_type=jnp.float32)
    mixed = mixed.reshape(row_count, model_width).astype(jnp.bfloat16)
    middle = (
        row_float
        + jnp.dot(mixed, outweight, preferred_element_type=jnp.float32)
        + outbias.astype(jnp.float32)
    )
    normed_mlp = layer_norm(
        middle, mlpgain.astype(jnp.float32), mlpbias.astype(jnp.float32)
    ).astype(jnp.bfloat16)
    hidden_pre = jnp.dot(normed_mlp, upweight, preferred_element_type=jnp.float32) + upbias.astype(
        jnp.float32
    )
    hidden = jax.nn.gelu(hidden_pre, approximate=False).astype(jnp.bfloat16)
    leaving = (
        middle
        + jnp.dot(hidden, downweight, preferred_element_type=jnp.float32)
        + downbias.astype(jnp.float32)
    )
    saved = (
        row_float,
        normed,
        head_q,
        head_k,
        head_v,
        scores,
        attn_low,
        mixed,
        middle,
        normed_mlp,
        hidden_pre,
        hidden,
    )
    return (leaving, saved)


def block_backward(weights, row_data, arriving, count_images):
    (
        normgain,
        normbias,
        qkvweight,
        qvbias,
        outweight,
        outbias,
        mlpgain,
        mlpbias,
        upweight,
        upbias,
        downweight,
        downbias,
    ) = weights
    saved = block_forward(weights, row_data, count_images)[1]
    (
        row_float,
        normed,
        head_q,
        head_k,
        head_v,
        scores,
        attn_low,
        mixed,
        middle,
        normed_mlp,
        hidden_pre,
        hidden,
    ) = saved
    row_count, model_width = row_data.shape
    qscale = HEAD ** (-0.5)
    down_grad = arriving.astype(jnp.bfloat16)
    grad_downbias = jnp.sum(down_grad, axis=0, dtype=jnp.float32)
    grad_downweight = jnp.einsum("rf,rd->fd", hidden, down_grad, preferred_element_type=jnp.float32)
    hidden_grad = jnp.einsum("rd,fd->rf", down_grad, downweight, preferred_element_type=jnp.float32)
    gelu_pull = jax.vjp(partial(jax.nn.gelu, approximate=False), hidden_pre)[1]
    up_grad = gelu_pull(hidden_grad)[0].astype(jnp.bfloat16)
    grad_upbias = jnp.sum(up_grad, axis=0, dtype=jnp.float32)
    grad_upweight = jnp.einsum("rd,rf->df", normed_mlp, up_grad, preferred_element_type=jnp.float32)
    normed_mlp_grad = jnp.einsum("rf,df->rd", up_grad, upweight, preferred_element_type=jnp.float32)
    mlp_pull = jax.vjp(
        layer_norm, middle, mlpgain.astype(jnp.float32), mlpbias.astype(jnp.float32)
    )[1]
    middle_part, grad_mlpgain, grad_mlpbias = mlp_pull(normed_mlp_grad)
    middle_grad = arriving + middle_part
    out_grad = middle_grad.astype(jnp.bfloat16)
    grad_outbias = jnp.sum(out_grad, axis=0, dtype=jnp.float32)
    grad_outweight = jnp.einsum("rd,re->de", mixed, out_grad, preferred_element_type=jnp.float32)
    mixed_grad = jnp.einsum("re,de->rd", out_grad, outweight, preferred_element_type=jnp.float32)
    mixed_grad = mixed_grad.astype(jnp.bfloat16).reshape(head_q.shape)
    attn_grad = jnp.einsum(
        "iqhd,ikhd->ihqk", mixed_grad, head_v, preferred_element_type=jnp.float32
    )
    values_grad = jnp.einsum(
        "ihqk,iqhd->ikhd", attn_low, mixed_grad, preferred_element_type=jnp.float32
    )
    values_grad = values_grad.reshape(row_count, model_width).astype(jnp.bfloat16)
    soft_pull = jax.vjp(softmax_rows, scores)[1]
    scores_grad = soft_pull(attn_grad)[0].astype(jnp.bfloat16)
    query_grad = jnp.einsum(
        "ihqk,ikhd->iqhd", scores_grad, head_k, preferred_element_type=jnp.float32
    )
    query_grad = query_grad.reshape(row_count, model_width).astype(jnp.bfloat16) * qscale
    keys_grad = jnp.einsum(
        "ihqk,iqhd->ikhd", scores_grad, head_q, preferred_element_type=jnp.float32
    )
    keys_grad = keys_grad.reshape(row_count, model_width).astype(jnp.bfloat16)
    joint_grad = jnp.concatenate([query_grad, keys_grad, values_grad], axis=1)
    grad_qvbias = jnp.concatenate(
        [
            jnp.sum(query_grad, axis=0, dtype=jnp.float32),
            jnp.sum(values_grad, axis=0, dtype=jnp.float32),
        ]
    )
    grad_qkvweight = jnp.einsum("rd,re->de", normed, joint_grad, preferred_element_type=jnp.float32)
    normed_grad = jnp.einsum("re,de->rd", joint_grad, qkvweight, preferred_element_type=jnp.float32)
    first_pull = jax.vjp(
        layer_norm, row_float, normgain.astype(jnp.float32), normbias.astype(jnp.float32)
    )[1]
    row_part, grad_normgain, grad_normbias = first_pull(normed_grad)
    entry_grad = middle_grad + row_part
    grads = (
        grad_normgain,
        grad_normbias,
        grad_qkvweight,
        grad_qvbias,
        grad_outweight,
        grad_outbias,
        grad_mlpgain,
        grad_mlpbias,
        grad_upweight,
        grad_upbias,
        grad_downweight,
        grad_downbias,
    )
    return (grads, entry_grad)


def row_weights(live_float, batch_id, token_count):
    slot_row = lax.dynamic_index_in_dim(live_float, batch_id, 0, keepdims=False)
    return jnp.repeat(slot_row, token_count)[:, None]


def place(store, item_rows, index, active):
    current = lax.dynamic_index_in_dim(store, index, 0, keepdims=False)
    return lax.dynamic_update_index_in_dim(store, jnp.where(active, item_rows, current), index, 0)


def body(
    images,
    cotangent,
    live_slots,
    normgain,
    normbias,
    qkvweight,
    qvbias,
    outweight,
    outbias,
    mlpgain,
    mlpbias,
    upweight,
    upbias,
    downweight,
    downbias,
):
    section_id = lax.axis_index("section")
    slot_count, token_count, model_width = images.shape
    per_batch = slot_count // MB
    batch_rows = per_batch * token_count
    live_float = live_slots.astype(jnp.float32).reshape(MB, per_batch)
    gathered = (
        lax.all_gather(normgain, "fsdp", axis=1, tiled=True),
        lax.all_gather(normbias, "fsdp", axis=1, tiled=True),
        lax.all_gather(qkvweight, "fsdp", axis=1, tiled=True),
        lax.all_gather(qvbias, "fsdp", axis=1, tiled=True),
        lax.all_gather(outweight, "fsdp", axis=1, tiled=True),
        lax.all_gather(outbias, "fsdp", axis=1, tiled=True),
        lax.all_gather(mlpgain, "fsdp", axis=1, tiled=True),
        lax.all_gather(mlpbias, "fsdp", axis=1, tiled=True),
        lax.all_gather(upweight, "fsdp", axis=1, tiled=True),
        lax.all_gather(upbias, "fsdp", axis=1, tiled=True),
        lax.all_gather(downweight, "fsdp", axis=1, tiled=True),
        lax.all_gather(downbias, "fsdp", axis=1, tiled=True),
    )
    weights_fwd = tuple((member[0] for member in gathered))
    incoming = jnp.zeros((batch_rows, model_width), jnp.bfloat16)
    kept_inputs = jnp.zeros((MB, batch_rows, model_width), jnp.bfloat16)
    exit_store = jnp.zeros((MB, batch_rows, model_width), jnp.bfloat16)
    for tick_num in range(MB + 1):
        offset = tick_num - section_id
        active = (offset >= 0) & (offset < MB)
        batch_id = jnp.clip(offset, 0, MB - 1)
        own_rows = lax.dynamic_index_in_dim(images, batch_id, 0, keepdims=False)
        entering = jnp.where(section_id == 0, own_rows, incoming)
        leaving = block_forward(weights_fwd, entering, per_batch)[0]
        row_mask = row_weights(live_float, batch_id, token_count)
        leaving_low = (leaving * row_mask).astype(jnp.bfloat16)
        kept_inputs = place(kept_inputs, entering, batch_id, active)
        exit_store = place(exit_store, leaving_low, batch_id, active)
        if tick_num < MB:
            incoming = from_behind(leaving_low, "section", 1)
    regathered = (
        lax.all_gather(normgain, "fsdp", axis=1, tiled=True),
        lax.all_gather(normbias, "fsdp", axis=1, tiled=True),
        lax.all_gather(qkvweight, "fsdp", axis=1, tiled=True),
        lax.all_gather(qvbias, "fsdp", axis=1, tiled=True),
        lax.all_gather(outweight, "fsdp", axis=1, tiled=True),
        lax.all_gather(outbias, "fsdp", axis=1, tiled=True),
        lax.all_gather(mlpgain, "fsdp", axis=1, tiled=True),
        lax.all_gather(mlpbias, "fsdp", axis=1, tiled=True),
        lax.all_gather(upweight, "fsdp", axis=1, tiled=True),
        lax.all_gather(upbias, "fsdp", axis=1, tiled=True),
        lax.all_gather(downweight, "fsdp", axis=1, tiled=True),
        lax.all_gather(downbias, "fsdp", axis=1, tiled=True),
    )
    weights_back = tuple((member[0] for member in regathered))
    totals = tuple((jnp.zeros(member.shape, jnp.float32) for member in weights_back))
    incoming_grad = jnp.zeros((batch_rows, model_width), jnp.bfloat16)
    entry_store = jnp.zeros((MB, batch_rows, model_width), jnp.bfloat16)
    for tick_num in range(MB + 1):
        offset = tick_num - (1 - section_id)
        active = (offset >= 0) & (offset < MB)
        batch_id = jnp.clip(offset, 0, MB - 1)
        own_grad = lax.dynamic_index_in_dim(cotangent, batch_id, 0, keepdims=False).astype(
            jnp.float32
        )
        row_mask = row_weights(live_float, batch_id, token_count) * active.astype(jnp.float32)
        arriving = (
            jnp.where(section_id == 1, own_grad, incoming_grad.astype(jnp.float32)) * row_mask
        )
        entering = lax.dynamic_index_in_dim(kept_inputs, batch_id, 0, keepdims=False)
        tick_grads, entry_grad = block_backward(weights_back, entering, arriving, per_batch)
        totals = tuple((total_now + extra for total_now, extra in zip(totals, tick_grads)))
        entry_low = entry_grad.astype(jnp.bfloat16)
        entry_store = place(entry_store, entry_low, batch_id, active)
        if tick_num < MB:
            incoming_grad = from_behind(entry_low, "section", -1)
    summed = (
        lax.psum_scatter(totals[0][None], "fsdp", scatter_dimension=1, tiled=True),
        lax.psum_scatter(totals[1][None], "fsdp", scatter_dimension=1, tiled=True),
        lax.psum_scatter(totals[2][None], "fsdp", scatter_dimension=1, tiled=True),
        lax.psum_scatter(totals[3][None], "fsdp", scatter_dimension=1, tiled=True),
        lax.psum_scatter(totals[4][None], "fsdp", scatter_dimension=1, tiled=True),
        lax.psum_scatter(totals[5][None], "fsdp", scatter_dimension=1, tiled=True),
        lax.psum_scatter(totals[6][None], "fsdp", scatter_dimension=1, tiled=True),
        lax.psum_scatter(totals[7][None], "fsdp", scatter_dimension=1, tiled=True),
        lax.psum_scatter(totals[8][None], "fsdp", scatter_dimension=1, tiled=True),
        lax.psum_scatter(totals[9][None], "fsdp", scatter_dimension=1, tiled=True),
        lax.psum_scatter(totals[10][None], "fsdp", scatter_dimension=1, tiled=True),
        lax.psum_scatter(totals[11][None], "fsdp", scatter_dimension=1, tiled=True),
    )
    exits = exit_store.reshape(1, slot_count, token_count, model_width)
    entries = entry_store.reshape(1, slot_count, token_count, model_width)
    return (
        exits,
        entries,
        summed[0],
        summed[1],
        summed[2],
        summed[3],
        summed[4],
        summed[5],
        summed[6],
        summed[7],
        summed[8],
        summed[9],
        summed[10],
        summed[11],
    )


def solution(mesh):
    in_specs = (
        P("fsdp", None, None),
        P("fsdp", None, None),
        P("fsdp"),
        P("section", "fsdp"),
        P("section", "fsdp"),
        P("section", "fsdp", None),
        P("section", "fsdp"),
        P("section", "fsdp", None),
        P("section", "fsdp"),
        P("section", "fsdp"),
        P("section", "fsdp"),
        P("section", "fsdp", None),
        P("section", "fsdp"),
        P("section", "fsdp", None),
        P("section", "fsdp"),
    )
    out_specs = (
        P("section", "fsdp", None, None),
        P("section", "fsdp", None, None),
        P("section", "fsdp"),
        P("section", "fsdp"),
        P("section", "fsdp", None),
        P("section", "fsdp"),
        P("section", "fsdp", None),
        P("section", "fsdp"),
        P("section", "fsdp"),
        P("section", "fsdp"),
        P("section", "fsdp", None),
        P("section", "fsdp"),
        P("section", "fsdp", None),
        P("section", "fsdp"),
    )
    return jax.shard_map(body, mesh=mesh, in_specs=in_specs, out_specs=out_specs, check_vma=False)
```

profile of v0, /device:TPU:0, one launch (start us, length us, event | category | flops | bytes accessed | tf_op | source)
XLA Modules:
  0.0 1572.9 jit_solution(4601117634872914116)
XLA Ops:
  20.7 63.9 %all-reduce.8 = (bf16[1536]{0:T(1024)(128)(2,1)S(1)}, bf16[768]{0:T(1024)(128)(2,1)S(1)}, bf16[768]{0:T(1024)(128)(2,1)S(1)}, bf16[768]{0:T(1024)(128)(2,1)S(1)}...) all-reduce(bf16[1536]{0:T(1024)(128)(2,1)S(1)} %dynamic-update-slic, ...), channel_id=1, replica_groups=mesh['section'=2,'fsdp'=16] {'fsdp'}, use_global_device_ids=true, to_apply=%add.2 | all-reduce | flops 9216 | bytes 36864
  85.5 8.0 constant_dynamic-slice_fusion.12
  105.5 48.9 %all-gather.11.cloned.1.call-done = bf16[1,3072,768]{2,1,0:T(8,128)(2,1)} async-done(((bf16[1,192,768]{2,1,0:T(8,128)(2,1)}), bf16[1,3072,768]{2,1,0:T(8,128)(2,1)}) %all-gather.11.cloned.1.call-update) | async-done | bytes 4718608 | tf_op jit(solution)/shard_map/all_gather | solution.py:244
  154.4 54.0 %all-gather.9.cloned.1.call-done = bf16[1,768,3072]{2,1,0:T(8,128)(2,1)} async-done(((bf16[1,48,3072]{2,1,0:T(8,128)(2,1)}), bf16[1,768,3072]{2,1,0:T(8,128)(2,1)}) %all-gather.9.cloned.1.call-update) | async-done | bytes 4718608 | tf_op jit(solution)/shard_map/all_gather | solution.py:242
  209.6 12.4 bitcast_dynamic-update-slice_fusion.11
  222.0 4.4 collective-permute-start
  228.2 4.7 collective-permute-done
  252.0 12.6 bitcast_dynamic-update-slice_fusion.10
  264.6 5.4 collective-permute-start.1
  294.6 12.6 bitcast_dynamic-update-slice_fusion.9
  307.2 5.6 collective-permute-start.2
  336.3 12.6 bitcast_dynamic-update-slice_fusion.8
  348.9 5.4 collective-permute-start.3
  354.3 7.7 constant_dynamic-slice_fusion
  397.5 10.3 convert_reduce_fusion.4
  465.8 9.1 convert_reduce_fusion.3
  474.9 5.2 multiply_reduce_fusion.8
  571.9 5.9 fusion.79
  584.2 7.9 convert_reduce_fusion.2
  627.4 9.2 convert_reduce_fusion.1
  636.7 5.2 multiply_reduce_fusion.6
  671.7 9.4 convert_reduce_fusion
  681.2 5.2 multiply_reduce_fusion.5
  715.8 5.4 add_bitcast_fusion.3
  725.1 4.1 fusion.691
  729.3 4.3 fusion.690
  733.6 4.2 fusion.689
  737.9 11.3 add_bitcast_fusion.2
  750.7 5.2 fusion.1062
  756.0 5.2 fusion.1063
  761.2 5.2 fusion.1064
  766.4 5.3 fusion.1065
  771.7 17.4 %add_bitcast_fusion.1 = f32[1,768,3072]{2,1,0:T(8,128)} fusion(f32[768,3072]{1,0:T(8,128)} %fusion.1065, f32[768,3072]{1,0:T(8,128)} %fusion.1064, f32[768,3072]{1,0:T(8,128)} %fusion.1062, f32[768,3072]{1,0:T(8,128)} %fusion.1063, bf16[197,3072]{1,0:T(8,128)(2,1)S(1)} %copy-done.143, f32[197,768]{1,0:T(8,128)S(1)} %copy-done.30, f32[768]{0:T(1024)S(1)} %add.1414, ...), kind=kOutput, calls=%fused_computation.6 | convolution fusion | flops 939756288 | bytes 49009192 | tf_op jit(solution)/shard_map/rd,rf->df/dot_general | solution.py:141
  791.0 8.8 fusion.300
  799.8 8.6 fusion.301
  808.4 8.6 fusion.302
  817.1 8.7 fusion.303
  825.7 18.8 %add_bitcast_fusion = f32[1,3072,768]{2,1,0:T(8,128)} fusion(f32[3072,768]{1,0:T(8,128)} %fusion.303, f32[3072,768]{1,0:T(8,128)} %fusion.302, f32[3072,768]{1,0:T(8,128)} %fusion.300, f32[3072,768]{1,0:T(8,128)} %fusion.301, bf16[197,768]{1,0:T(8,128)(2,1)S(1)} %copy-done.194, f32[197,3072]{1,0:T(8,128)S(1)} %copy-done.97), kind=kOutput, calls=%fused_computation.5 | convolution fusion | flops 978336768 | bytes 49909248 | tf_op jit(solution)/shard_map/rf,rd->fd/dot_general | solution.py:136
  854.3 11.8 fusion.514
  878.5 57.2 %reduce-scatter.45.cloned.1.call-done = f32[48,1]{1,0:T(8,128)} async-done(((f32[768,1]{1,0:T(8,128)}), f32[48,1]{1,0:T(8,128)}) %reduce-scatter.45.cloned.1.call-update) | async-done | bytes 208
  937.1 56.9 %reduce-scatter.47.cloned.1.call-done = f32[48,1]{1,0:T(8,128)} async-done(((f32[768,1]{1,0:T(8,128)}), f32[48,1]{1,0:T(8,128)}) %reduce-scatter.47.cloned.1.call-update) | async-done | bytes 208
  995.3 57.1 %reduce-scatter.51.cloned.1.call-done = f32[48,1]{1,0:T(8,128)} async-done(((f32[768,1]{1,0:T(8,128)}), f32[48,1]{1,0:T(8,128)}) %reduce-scatter.51.cloned.1.call-update) | async-done | bytes 208
  1053.7 57.8 %reduce-scatter.41.cloned.1.call-done = f32[96,1]{1,0:T(8,128)} async-done(((f32[1536,1]{1,0:T(8,128)}), f32[96,1]{1,0:T(8,128)}) %reduce-scatter.41.cloned.1.call-update) | async-done | bytes 400
  1112.9 61.1 %reduce-scatter.49.cloned.1.call-done = f32[192,1]{1,0:T(8,128)} async-done(((f32[3072,1]{1,0:T(8,128)}), f32[192,1]{1,0:T(8,128)}) %reduce-scatter.49.cloned.1.call-update) | async-done | bytes 784
  1175.6 64.8 %reduce-scatter.31.cloned.1.call-done = f32[1,48,768]{2,1,0:T(8,128)} async-done(((f32[1,768,768]{2,1,0:T(8,128)}), f32[1,48,768]{2,1,0:T(8,128)}) %reduce-scatter.31.cloned.1.call-update) | async-done | bytes 147472 | tf_op jit(solution)/shard_map/reduce_scatter | solution.py:305
  1240.4 94.1 %reduce-scatter.29.cloned.1.call-done = f32[1,48,2304]{2,1,0:T(8,128)} async-done(((f32[1,768,2304]{2,1,0:T(8,128)}), f32[1,48,2304]{2,1,0:T(8,128)}) %reduce-scatter.29.cloned.1.call-update) | async-done | bytes 442384 | tf_op jit(solution)/shard_map/reduce_scatter | solution.py:303
  1334.5 115.4 %reduce-scatter.33.cloned.1.call-done = f32[1,48,3072]{2,1,0:T(8,128)} async-done(((f32[1,768,3072]{2,1,0:T(8,128)}), f32[1,48,3072]{2,1,0:T(8,128)}) %reduce-scatter.33.cloned.1.call-update) | async-done | bytes 589840 | tf_op jit(solution)/shard_map/reduce_scatter | solution.py:309
  1449.9 116.2 %reduce-scatter.35.cloned.1.call-done = f32[1,192,768]{2,1,0:T(8,128)} async-done(((f32[1,3072,768]{2,1,0:T(8,128)}), f32[1,192,768]{2,1,0:T(8,128)}) %reduce-scatter.35.cloned.1.call-update) | async-done | bytes 589840 | tf_op jit(solution)/shard_map/reduce_scatter | solution.py:311
  (1160 shorter events, 410.0 us)
Async XLA Ops:
  7.2 86.9 %all-gather.5.cloned.1.call-start = ((), (), s32[]{:S(2)}) async-start(), calls=%async_computation.12 | async-start | bytes 3760128 | tf_op jit(solution)/shard_map/all_gather | solution.py:236
  7.9 95.5 %all-gather.7.cloned.1.call-start = ((), (), s32[]{:S(2)}) async-start(), calls=%async_computation.13 | async-start | bytes 1253376 | tf_op jit(solution)/shard_map/all_gather | solution.py:238
  8.7 145.8 %all-gather.11.cloned.1.call-start = ((), (), s32[]{:S(2)}) async-start(), calls=%async_computation.15 | async-start | bytes 5013504 | tf_op jit(solution)/shard_map/all_gather | solution.py:244
  9.4 199.0 %all-gather.9.cloned.1.call-start = ((), (), s32[]{:S(2)}) async-start(), calls=%async_computation.14 | async-start | bytes 5013504 | tf_op jit(solution)/shard_map/all_gather | solution.py:242
  10.0 861.1 %reduce-scatter.37.cloned.1.call-start = ((), (), s32[]{:S(2)}) async-start(), calls=%async_computation.20 | async-start | bytes 417792
  84.6 125.0 %copy-start.356 = (f32[768]{0:T(1024)}, f32[768]{0:T(1024)S(1)}, u32[]{:S(2)}) copy-start(f32[768]{0:T(1024)S(1)} %add.1416) | copy-start | bytes 9220
  84.7 18.8 %copy-start.158 = (f32[768]{0:T(1024)}, f32[768]{0:T(1024)S(1)}, u32[]{:S(2)}) copy-start(f32[768]{0:T(1024)S(1)} %add.1413) | copy-start | bytes 9220
  84.7 653.2 %copy-start.56 = (f32[768]{0:T(1024)}, f32[768]{0:T(1024)S(1)}, u32[]{:S(2)}) copy-start(f32[768]{0:T(1024)S(1)} %mul.1661) | copy-start | bytes 9220
  84.7 124.9 %copy-start.163 = (f32[3072]{0:T(1024)}, f32[3072]{0:T(1024)S(1)}, u32[]{:S(2)}) copy-start(f32[3072]{0:T(1024)S(1)} %add.1415) | copy-start | bytes 36868
  85.5 12.4 copy-start.195
  85.5 12.4 copy-start.202
  222.0 13.2 copy-start
  222.0 10.9 collective-permute-start
  264.6 10.9 collective-permute-start.1
  307.2 10.0 collective-permute-start.2
  348.9 19.8 %collective-permute-start.3 = (bf16[197,768]{1,0:T(8,128)(2,1)}, bf16[197,768]{1,0:T(8,128)(2,1)}, u32[]{:S(2)}, u32[]{:S(2)}) collective-permute-start(bf16[197,768]{1,0:T(8,128)(2,1)} %get-tuple-element.252), channel_id=1, source_target_pairs={{0,16},{1,17},{2,18},{3,19},{4,20},{5,21},{6,22},{7,23},{8,24},{9,... | collective-permute-start | bytes 907784 | tf_op jit(solution)/shard_map/ppermute | solution.py:19
  393.4 16.7 %copy-start.31 = (f32[197,768]{1,0:T(8,128)}, f32[197,768]{1,0:T(8,128)S(1)}, u32[]{:S(2)}) copy-start(f32[197,768]{1,0:T(8,128)S(1)} %get-tuple-element.256) | copy-start | bytes 1815556
  393.4 16.7 %copy-start.252 = (f32[197]{0:T(256)}, f32[197]{0:T(256)S(1)}, u32[]{:S(2)}) copy-start(f32[197]{0:T(256)S(1)} %broadcast_multiply_fusion.8) | copy-start | bytes 2368
  393.7 16.5 %copy-start.269 = (f32[197]{0:T(256)}, f32[197]{0:T(256)S(1)}, u32[]{:S(2)}) copy-start(f32[197]{0:T(256)S(1)} %fusion.860) | copy-start | bytes 2368
  393.7 14.1 slice-start
  397.4 10.3 copy-start.92
  397.4 10.3 slice-start.1
  444.5 10.2 slice-start.2
  449.4 14.7 collective-permute-start.4
  549.3 33.1 %collective-permute-start.5 = (bf16[197,768]{1,0:T(8,128)(2,1)}, bf16[197,768]{1,0:T(8,128)(2,1)}, u32[]{:S(2)}, u32[]{:S(2)}) collective-permute-start(bf16[197,768]{1,0:T(8,128)(2,1)} %get-tuple-element.153), channel_id=1, source_target_pairs={{16,0},{17,1},{18,2},{19,3},{20,4},{21,5},{22,6},{23,7},{24,8},{25... | collective-permute-start | bytes 907784 | tf_op jit(solution)/shard_map/ppermute | solution.py:19
  567.9 9.9 slice-start.4
  571.9 12.3 copy-start.100
  571.9 12.2 slice-start.6
  615.2 10.5 collective-permute-start.6
  627.4 9.3 copy-start.266
  627.4 9.3 copy-start.277
  660.9 9.1 collective-permute-start.7
  671.7 9.5 copy-start.193
  671.7 9.5 copy-start.29
  671.7 9.5 copy-start.281
  671.7 9.5 copy-start.288
  706.1 166.3 %reduce-scatter.39.cloned.1.call-start = ((), (), s32[]{:S(2)}) async-start(), calls=%async_computation.21 | async-start | bytes 417792
  707.8 169.4 %reduce-scatter.43.cloned.1.call-start = ((), (), s32[]{:S(2)}) async-start(), calls=%async_computation.23 | async-start | bytes 417792
  708.9 226.8 %reduce-scatter.45.cloned.1.call-start = ((), (), s32[]{:S(2)}) async-start(), calls=%async_computation.24 | async-start | bytes 417792
  710.0 284.0 %reduce-scatter.47.cloned.1.call-start = ((), (), s32[]{:S(2)}) async-start(), calls=%async_computation.25 | async-start | bytes 417792
  711.0 341.4 %reduce-scatter.51.cloned.1.call-start = ((), (), s32[]{:S(2)}) async-start(), calls=%async_computation.27 | async-start | bytes 417792
  712.3 399.3 %reduce-scatter.41.cloned.1.call-start = ((), (), s32[]{:S(2)}) async-start(), calls=%async_computation.22 | async-start | bytes 835584
  713.6 460.4 %reduce-scatter.49.cloned.1.call-start = ((), (), s32[]{:S(2)}) async-start(), calls=%async_computation.26 | async-start | bytes 1671168
  715.5 524.9 %reduce-scatter.31.cloned.1.call-start = ((), (), s32[]{:S(2)}) async-start(), calls=%async_computation.17 | async-start | bytes 2506752 | tf_op jit(solution)/shard_map/reduce_scatter | solution.py:305
  721.2 613.3 %reduce-scatter.29.cloned.1.call-start = ((), (), s32[]{:S(2)}) async-start(), calls=%async_computation.16 | async-start | bytes 7520256 | tf_op jit(solution)/shard_map/reduce_scatter | solution.py:303
  749.3 700.6 %reduce-scatter.33.cloned.1.call-start = ((), (), s32[]{:S(2)}) async-start(), calls=%async_computation.18 | async-start | bytes 10027008 | tf_op jit(solution)/shard_map/reduce_scatter | solution.py:309
  789.2 10.6 copy-start.188
  789.2 777.0 %reduce-scatter.35.cloned.1.call-start = ((), (), s32[]{:S(2)}) async-start(), calls=%async_computation.19 | async-start | bytes 10027008 | tf_op jit(solution)/shard_map/reduce_scatter | solution.py:311
  (353 other events, 1247.6 us)
Sparse Core Ops, SparseCore 0:
  10.3 49.9 all-gather.4
  62.6 37.2 all-gather.6
  102.2 52.1 all-gather.10
  156.6 51.7 all-gather.8
  706.2 54.3 reduce-scatter.36
  764.3 54.6 reduce-scatter.38
  822.5 54.6 reduce-scatter.42
  881.1 54.6 reduce-scatter.44
  939.3 54.6 reduce-scatter.46
  997.7 54.6 reduce-scatter.50
  1056.0 55.5 reduce-scatter.40
  1115.5 58.5 reduce-scatter.48
  1178.4 61.9 reduce-scatter.30
  1245.3 89.1 reduce-scatter.28
  1339.0 110.8 reduce-scatter.32
  1455.0 111.1 reduce-scatter.34
where the time goes:
time: 1580 us; the launch traced here: 1570 us
  waiting for transfers between devices  804 us (51%)
  matrix products  408 us (26%)
  local copies, waits for them, and re-layouts  161 us (10%)
  other arithmetic  85 us (5%)
  blocking collectives  63.9 us (4%)
  starting transfers between devices  27.1 us (2%)
  between operations  23.8 us (2%)
    unnamed x24, waiting for transfers between devices  296 us
    reduce_scatter x1, waiting for transfers between devices, body(): lax.psum_scatter(totals[10][None], 'fsdp', scatter_dimension=1, tiled=True)  116 us
    reduce_scatter x1, waiting for transfers between devices, body(): lax.psum_scatter(totals[8][None], 'fsdp', scatter_dimension=1, tiled=True)  115 us
    reduce_scatter x1, waiting for transfers between devices, body(): lax.psum_scatter(totals[2][None], 'fsdp', scatter_dimension=1, tiled=True)  94.1 us
    reduce_scatter x1, waiting for transfers between devices, body(): lax.psum_scatter(totals[4][None], 'fsdp', scatter_dimension=1, tiled=True)  64.8 us
    unnamed x1, blocking collectives  63.9 us
    dot_general x5, matrix products, block_forward(): jnp.dot(hidden, downweight, preferred_element_type=jnp.float32)  62 us
    all_gather x1, waiting for transfers between devices, body(): lax.all_gather(upweight, 'fsdp', axis=1, tiled=True)  54 us
  transfers between devices with their start and end apart: 24, of which 17 were waited for; matrix products, arithmetic and copies ran while one was open for 17% of the time, Pallas kernels for 0%

commit v1 on v0

v1 whole, which is shorter than its diff:
```python
import jax
import jax.numpy as jnp
from jax import lax
from jax.experimental import pallas as pl
from jax.experimental.pallas import tpu as pltpu
from jax.sharding import PartitionSpec as P

HEADS = 12
HEAD = 64
EPSILON = 1e-06
F32 = jnp.float32
BF16 = jnp.bfloat16


def dot(left, right, left_dim=1, right_dim=0):
    dims = (((left_dim,), (right_dim,)), ((), ()))
    return lax.dot_general(left, right, dims, preferred_element_type=F32)


def head_masks():
    lane = lax.broadcasted_iota(jnp.int32, (1, 2 * HEAD), 1)
    first = (lane < HEAD).astype(F32)
    return first.astype(BF16), (1.0 - first).astype(BF16)


def attention_rows(scores, tokens):
    column = lax.broadcasted_iota(jnp.int32, scores.shape, 1)
    scores = jnp.where(column < tokens, scores, -1e30)
    expo = jnp.exp(scores - jnp.max(scores, axis=-1, keepdims=True))
    return expo * (1.0 / jnp.sum(expo, axis=-1, keepdims=True))


def attend_kernel(tokens, width, joint_ref, mixed_ref):
    masks = head_masks()
    for start in range(0, width, 2 * HEAD):
        pair = slice(start, start + 2 * HEAD)
        queries = joint_ref[:, pair]
        keys = joint_ref[:, width + start : width + start + 2 * HEAD]
        values = joint_ref[:, 2 * width + start : 2 * width + start + 2 * HEAD]
        mixed = 0.0
        for mask in masks:
            attn = attention_rows(dot(queries * mask, keys, 1, 1), tokens).astype(BF16)
            mixed = mixed + dot(attn, values * mask)
        mixed_ref[:, pair] = mixed.astype(BF16)


def attend_back_kernel(tokens, width, joint_ref, mixed_grad_ref, joint_grad_ref):
    masks = head_masks()
    for start in range(0, width, 2 * HEAD):
        pair = slice(start, start + 2 * HEAD)
        key_pair = slice(width + start, width + start + 2 * HEAD)
        value_pair = slice(2 * width + start, 2 * width + start + 2 * HEAD)
        queries = joint_ref[:, pair]
        keys = joint_ref[:, key_pair]
        values = joint_ref[:, value_pair]
        mixed_grad = mixed_grad_ref[:, pair]
        query_grad = 0.0
        keys_grad = 0.0
        values_grad = 0.0
        for mask in masks:
            head_q = queries * mask
            head_g = mixed_grad * mask
            attn = attention_rows(dot(head_q, keys, 1, 1), tokens)
            attn_grad = dot(head_g, values, 1, 1)
            values_grad = values_grad + dot(attn.astype(BF16), head_g, 0, 0)
            inner = jnp.sum(attn * attn_grad, axis=-1, keepdims=True)
            scores_grad = (attn * (attn_grad - inner)).astype(BF16)
            query_grad = query_grad + dot(scores_grad, keys * mask)
            keys_grad = keys_grad + dot(scores_grad, head_q, 0, 0)
        scaled = query_grad.astype(BF16).astype(F32) * HEAD ** (-0.5)
        joint_grad_ref[:, pair] = scaled.astype(BF16)
        joint_grad_ref[:, key_pair] = keys_grad.astype(BF16)
        joint_grad_ref[:, value_pair] = values_grad.astype(BF16)


def attend(joint, tokens):
    rows, width = joint.shape[0], joint.shape[1] // 3
    return pl.pallas_call(
        lambda *refs: attend_kernel(tokens, width, *refs),
        out_shape=jax.ShapeDtypeStruct((rows, width), BF16),
        name="attend",
        compiler_params=pltpu.CompilerParams(vmem_limit_bytes=24 * 2**20),
        cost_estimate=pl.CostEstimate(
            flops=4 * rows * rows * width * 2,
            bytes_accessed=8 * rows * width,
            transcendentals=HEADS * rows * rows,
        ),
    )(joint)


def attend_back(joint, mixed_grad, tokens):
    rows, width = mixed_grad.shape
    return pl.pallas_call(
        lambda *refs: attend_back_kernel(tokens, width, *refs),
        out_shape=jax.ShapeDtypeStruct((rows, 3 * width), BF16),
        name="attend_back",
        compiler_params=pltpu.CompilerParams(vmem_limit_bytes=24 * 2**20),
        cost_estimate=pl.CostEstimate(
            flops=10 * rows * rows * width * 2,
            bytes_accessed=14 * rows * width,
            transcendentals=HEADS * rows * rows,
        ),
    )(joint, mixed_grad)


def unit_rows(row_data):
    center = row_data - jnp.mean(row_data, axis=-1, keepdims=True)
    spread = jnp.mean(center * center, axis=-1, keepdims=True)
    inverse = lax.rsqrt(spread + EPSILON)
    return center * inverse, inverse


def norm_back(row_data, gain_row, grad):
    unit, inverse = unit_rows(row_data)
    scaled = grad * gain_row
    first = jnp.mean(scaled, axis=-1, keepdims=True)
    second = jnp.mean(scaled * unit, axis=-1, keepdims=True)
    row_grad = inverse * (scaled - first - unit * second)
    return row_grad, jnp.sum(grad * unit, axis=0), jnp.sum(grad, axis=0)


def block_forward(small, large, entering, tokens):
    normgain, normbias, qvbias, outbias, mlpgain, mlpbias, upbias, downbias = small
    qkvweight, outweight, upweight, downweight = large
    width = entering.shape[1]
    row_float = entering.astype(F32)
    normed = (unit_rows(row_float)[0] * normgain + normbias).astype(BF16)
    bias = jnp.concatenate([qvbias[:width], jnp.zeros((width,), F32), qvbias[width:]])
    scale = jnp.where(jnp.arange(3 * width) < width, HEAD ** (-0.5), 1.0)
    joint = ((dot(normed, qkvweight) + bias) * scale).astype(BF16)
    mixed = attend(joint, tokens)
    middle = row_float + dot(mixed, outweight) + outbias
    normed_mlp = (unit_rows(middle)[0] * mlpgain + mlpbias).astype(BF16)
    pre = dot(normed_mlp, upweight) + upbias
    chance = 0.5 + 0.5 * lax.erf(pre * 0.5**0.5)
    density = jnp.exp(-0.5 * pre * pre) * 0.3989422804014327
    hidden = (pre * chance).astype(BF16)
    slope = (chance + pre * density).astype(BF16)
    hidden, slope = lax.optimization_barrier((hidden, slope))
    leaving = middle + dot(hidden, downweight) + downbias
    return leaving, (entering, normed, joint, mixed, middle, normed_mlp, hidden, slope)


def block_backward(small, large, saved, arriving, tokens):
    normgain, mlpgain = small[0], small[4]
    qkvweight, outweight, upweight, downweight = large
    entering, normed, joint, mixed, middle, normed_mlp, hidden, slope = saved
    down_grad = arriving.astype(BF16)
    up_grad = (dot(down_grad, downweight, 1, 1) * slope.astype(F32)).astype(BF16)
    up_grad = lax.optimization_barrier(up_grad)
    part, grad_mlpgain, grad_mlpbias = norm_back(middle, mlpgain, dot(up_grad, upweight, 1, 1))
    middle_grad = arriving + part
    out_grad = middle_grad.astype(BF16)
    mixed_grad = dot(out_grad, outweight, 1, 1).astype(BF16)
    joint_grad = attend_back(joint, mixed_grad, tokens)
    part, grad_normgain, grad_normbias = norm_back(
        entering.astype(F32), normgain, dot(joint_grad, qkvweight, 1, 1)
    )
    sums = (grad_normgain, grad_normbias, grad_mlpgain, grad_mlpbias)
    return middle_grad + part, sums, (down_grad, up_grad, out_grad, joint_grad)


def body(
    images,
    cotangent,
    live_slots,
    normgain,
    normbias,
    qkvweight,
    qvbias,
    outweight,
    outbias,
    mlpgain,
    mlpbias,
    upweight,
    upbias,
    downweight,
    downbias,
):
    section_id = lax.axis_index("section")
    peers = lax.axis_size("fsdp")
    batches, tokens, width = images.shape
    rows = -(-tokens // 16) * 16
    padding = ((0, 0), (0, rows - tokens), (0, 0))
    live = live_slots.astype(F32)

    shards = (normgain, normbias, qvbias, outbias, mlpgain, mlpbias, upbias, downbias)
    lengths = [member.shape[1] for member in shards]
    packed = jnp.concatenate([member[0].astype(F32) for member in shards])
    room = -(-packed.shape[0] // 1024) * 1024
    packed = jnp.pad(packed, (0, room - packed.shape[0])).reshape(room // 128, 128)
    packed = lax.all_gather(packed, "fsdp", axis=0, tiled=True).reshape(peers, room)
    small = []
    at = 0
    for length in lengths:
        small.append(packed[:, at : at + length].reshape(-1))
        at += length
    large = tuple(
        lax.all_gather(member[0], "fsdp", axis=0, tiled=True)
        for member in (qkvweight, outweight, upweight, downweight)
    )
    images = jnp.pad(images, padding)
    cotangent = jnp.pad(cotangent, padding)

    ticks = batches + 1
    incoming = jnp.zeros((rows, width), BF16)
    kept = []
    leavings = []
    for tick in range(ticks):
        here, there = min(tick, batches - 1), max(tick - 1, 0)
        entering = jnp.where(section_id == 0, images[here], incoming)
        leaving, saved = block_forward(small, large, entering, tokens)
        alive = jnp.where(section_id == 0, live[here], live[there])
        leaving_low = (leaving * alive).astype(BF16)
        kept.append(saved)
        leavings.append(leaving_low)
        if tick < batches:
            incoming = lax.ppermute(leaving_low, "section", [(0, 1)])

    incoming = jnp.zeros((rows, width), BF16)
    entries = [None] * ticks
    grads = [None] * ticks
    sums = None
    real_row = (jnp.arange(rows) < tokens)[:, None].astype(F32)
    for tick in reversed(range(ticks)):
        here, there = min(tick, batches - 1), max(tick - 1, 0)
        alive_here = live[here] if tick < batches else 0.0
        alive_there = live[there] if tick > 0 else 0.0
        alive = jnp.where(section_id == 0, alive_here, alive_there)
        own = jnp.where(section_id == 1, cotangent[there], incoming).astype(F32)
        arriving = own * (alive * real_row)
        entry, tick_sums, grads[tick] = block_backward(small, large, kept[tick], arriving, tokens)
        entries[tick] = entry.astype(BF16)
        sums = tick_sums if sums is None else tuple(a + b for a, b in zip(sums, tick_sums))
        if tick > 0:
            incoming = lax.ppermute(entries[tick], "section", [(1, 0)])

    def joined(members):
        return jnp.concatenate(members, axis=0)

    down_grad, up_grad, out_grad, joint_grad = (joined(m) for m in zip(*grads))
    _, normed, _, mixed, _, normed_mlp, hidden, _ = zip(*kept)

    def spread(left, right):
        total = dot(joined(left), right, 0, 0).astype(BF16)
        return lax.psum_scatter(total, "fsdp", scatter_dimension=0, tiled=True).astype(F32)[None]

    down_sum = spread(hidden, down_grad)
    up_sum = spread(normed_mlp, up_grad)
    out_sum = spread(mixed, out_grad)
    qkv_sum = spread(normed, joint_grad)

    def rows_sum(member):
        return jnp.sum(member.astype(F32), axis=0)

    joint_sum = rows_sum(joint_grad)
    vectors = (
        sums[0],
        sums[1],
        jnp.concatenate([joint_sum[:width], joint_sum[2 * width :]]),
        rows_sum(out_grad),
        sums[2],
        sums[3],
        rows_sum(up_grad),
        rows_sum(down_grad),
    )
    packed = jnp.concatenate([vector.reshape(peers, -1) for vector in vectors], axis=1)
    packed = jnp.pad(packed, ((0, 0), (0, room - packed.shape[1])))
    packed = packed.reshape(peers * room // 128, 128)
    packed = lax.psum_scatter(packed, "fsdp", scatter_dimension=0, tiled=True).reshape(1, room)
    outs = []
    at = 0
    for length in lengths:
        outs.append(packed[:, at : at + length])
        at += length

    def by_batch(members):
        return jnp.stack(
            [
                jnp.where(section_id == 0, members[b][:tokens], members[b + 1][:tokens])
                for b in range(batches)
            ]
        )[None]

    return (
        by_batch(leavings),
        by_batch(entries),
        outs[0],
        outs[1],
        qkv_sum,
        outs[2],
        out_sum,
        outs[3],
        outs[4],
        outs[5],
        up_sum,
        outs[6],
        down_sum,
        outs[7],
    )


def solution(mesh):
    in_specs = (
        P("fsdp", None, None),
        P("fsdp", None, None),
        P("fsdp"),
        P("section", "fsdp"),
        P("section", "fsdp"),
        P("section", "fsdp", None),
        P("section", "fsdp"),
        P("section", "fsdp", None),
        P("section", "fsdp"),
        P("section", "fsdp"),
        P("section", "fsdp"),
        P("section", "fsdp", None),
        P("section", "fsdp"),
        P("section", "fsdp", None),
        P("section", "fsdp"),
    )
    out_specs = (
        P("section", "fsdp", None, None),
        P("section", "fsdp", None, None),
        P("section", "fsdp"),
        P("section", "fsdp"),
        P("section", "fsdp", None),
        P("section", "fsdp"),
        P("section", "fsdp", None),
        P("section", "fsdp"),
        P("section", "fsdp"),
        P("section", "fsdp"),
        P("section", "fsdp", None),
        P("section", "fsdp"),
        P("section", "fsdp", None),
        P("section", "fsdp"),
    )
    return jax.shard_map(body, mesh=mesh, in_specs=in_specs, out_specs=out_specs, check_vma=False)
```

time: 1580 us -> 829 us (0.52)
  waiting for transfers between devices: 804 us -> 507 us
  matrix products: 408 us -> 123 us
  local copies, waits for them, and re-layouts: 161 us -> 39.1 us
  blocking collectives: 63.9 us -> 23.4 us
  other arithmetic: 85 us -> 49.6 us
  Pallas kernels: 0 us -> 32.7 us
    unnamed x24 -> x10, waiting for transfers between devices: 296 us -> 24 us
    dot_general x105 -> x44, matrix products: 391 us -> 123 us  [dot(): return lax.dot_general(left, right, dims, preferred_element_type=F32)]
    reduce_scatter x4, waiting for transfers between devices: 391 us -> 285 us  [spread(): lax.psum_scatter(total, 'fsdp', scatter_dimension=0, tiled=True).astype(F32)]
    unnamed x1 -> x0, blocking collectives: 63.9 us -> none
    all_gather x4, waiting for transfers between devices: 103 us -> 154 us  [body(): lax.all_gather(member[0], 'fsdp', axis=0, tiled=True)]
    convert_element_type x26 -> x0, local copies, waits for them, and re-layouts: 41 us -> none  [the longest x10 16.2 us: block_forward(): (joint[:, 2 * model_width:] + bias_float[model_width:]).astype(jnp.bfloat16)]
    reduce_sum x57 -> x19, other arithmetic: 50.8 us -> 17 us  [the longest x4 10.6 us: rows_sum(): return jnp.sum(member.astype(F32), axis=0)]
    pallas_call x0 -> x10, Pallas kernels: none -> 32.7 us  [the longest x5 24.3 us: attend_back(): pl.pallas_call(lambda *refs: attend_back_kernel(tokens, width, *refs), ou...]
  transfers between devices with their start and end apart: 24 -> 17, of which waited for: 17 -> 17; matrix products, arithmetic and copies ran while one was open for 17% -> 10% of each run, Pallas kernels for 0% -> 0%
where the time goes in v1:
time: 829 us; the launch traced here: 823 us
  waiting for transfers between devices  507 us (61%)
  matrix products  123 us (15%)
  other arithmetic  49.6 us (6%)
  local copies, waits for them, and re-layouts  39.1 us (5%)
  Pallas kernels  32.7 us (4%)
  starting transfers between devices  24.6 us (3%)
  blocking collectives  23.4 us (3%)
  between operations  22.9 us (3%)
    reduce_scatter x4, waiting for transfers between devices, spread(): lax.psum_scatter(total, 'fsdp', scatter_dimension=0, tiled=True).astype(F32)  285 us
    all_gather x4, waiting for transfers between devices, body(): lax.all_gather(member[0], 'fsdp', axis=0, tiled=True)  154 us
    dot_general x44, matrix products, dot(): return lax.dot_general(left, right, dims, preferred_element_type=F32)  123 us
    ppermute x4, waiting for transfers between devices, body(): incoming = lax.ppermute(entries[tick], 'section', [(1, 0)])  27.7 us
    unnamed x396, local copies, waits for them, and re-layouts  27.4 us
    pallas_call x5, Pallas kernels, attend_back(): pl.pallas_call(lambda *refs: attend_back_kernel(tokens, width, *refs), ou...  24.3 us
    unnamed x10, waiting for transfers between devices  24 us
    all_gather x1, blocking collectives, body(): lax.all_gather(packed, 'fsdp', axis=0, tiled=True).reshape(peers, room)  23.4 us
  transfers between devices with their start and end apart: 17, of which 17 were waited for; matrix products, arithmetic and copies ran while one was open for 10% of the time, Pallas kernels for 0%

profile of v1, /device:TPU:0, one launch (start us, length us, event | category | flops | bytes accessed | tf_op | source)
XLA Modules:
  0.0 822.7 jit_solution(1884987631438338023)
XLA Ops:
  10.7 4.8 concatenate.46
  15.5 23.4 %all_gather.15 = f32[128,128]{1,0:T(8,128)S(1)} all-gather(f32[8,128]{1,0:T(8,128)S(1)} %bitcast_convert_fusion.4), channel_id=1, replica_groups=mesh['section'=2,'fsdp'=16] {'fsdp'}, dimensions={0}, use_global_device_ids=true | all-gather | bytes 69632 | tf_op jit(solution)/shard_map/all_gather | solution.py:192
  41.0 19.3 %all-gather.9.cloned.1.call-done = bf16[1,768,2304]{2,1,0:T(8,128)(2,1)} async-done(((bf16[1,48,2304]{2,1,0:T(8,128)(2,1)}), bf16[1,768,2304]{2,1,0:T(8,128)(2,1)}) %all-gather.9.cloned.1.call-update) | async-done | bytes 3538960 | tf_op jit(solution)/shard_map/all_gather | solution.py:199
  60.3 3.0 fusion.90.refs_0_
  65.0 34.9 %all-gather.11.cloned.1.call-done = bf16[1,768,768]{2,1,0:T(8,128)(2,1)} async-done(((bf16[1,48,768]{2,1,0:T(8,128)(2,1)}), bf16[1,768,768]{2,1,0:T(8,128)(2,1)}) %all-gather.11.cloned.1.call-update) | async-done | bytes 1179664 | tf_op jit(solution)/shard_map/all_gather | solution.py:199
  102.0 52.4 %all-gather.13.cloned.1.call-done = bf16[1,768,3072]{2,1,0:T(8,128)(2,1)} async-done(((bf16[1,48,3072]{2,1,0:T(8,128)(2,1)}), bf16[1,768,3072]{2,1,0:T(8,128)(2,1)}) %all-gather.13.cloned.1.call-update) | async-done | bytes 4718608 | tf_op jit(solution)/shard_map/all_gather | solution.py:199
  154.4 6.2 fusion.114
  160.7 47.7 %all-gather.15.cloned.1.call-done = bf16[1,3072,768]{2,1,0:T(8,128)(2,1)} async-done(((bf16[1,192,768]{2,1,0:T(8,128)(2,1)}), bf16[1,3072,768]{2,1,0:T(8,128)(2,1)}) %all-gather.15.cloned.1.call-update) | async-done | bytes 4718608 | tf_op jit(solution)/shard_map/all_gather | solution.py:199
  208.4 4.5 fusion.185
  213.0 3.6 collective-permute-start
  217.9 5.7 collective-permute-done
  224.0 3.5 fusion.91.refs_0_
  230.0 3.8 fusion.119
  235.1 4.4 collective-permute-start.1
  240.8 5.1 collective-permute-done.1
  247.5 3.1 fusion.92.refs_0_
  253.2 3.7 fusion.124
  258.1 4.8 collective-permute-start.2
  264.2 3.7 collective-permute-done.2
  270.2 3.1 fusion.93.refs_0_
  275.9 3.8 fusion.129
  281.7 4.4 collective-permute-start.3
  286.7 2.5 copy.34
  292.5 3.1 fusion.94.refs_0_
  298.2 4.0 fusion.134
  307.1 4.9 attend_back.5
  317.2 7.0 collective-permute-done.4
  325.4 4.5 fusion.84
  330.0 5.3 multiply_reduce_fusion.3
  337.2 4.9 attend_back.6
  347.1 6.4 collective-permute-done.5
  359.0 4.9 attend_back.7
  368.1 7.0 collective-permute-done.6
  380.2 4.9 attend_back.8
  388.6 7.3 collective-permute-done.7
  403.3 4.9 attend_back.9
  415.8 3.2 convert_reduce_fusion.1
  429.1 3.8 convert_reduce_fusion
  439.4 4.3 convolution_convert_fusion.3
  447.6 9.4 %convolution_convert_fusion = bf16[768,2304]{1,0:T(8,128)(2,1)} fusion(bf16[1040,768]{1,0:T(8,128)(2,1)} %constant_dynamic-update-slice_fusion.10, bf16[1040,2304]{1,0:T(8,128)(2,1)} %constant_dynamic-update-slice_fusion), kind=kOutput, calls=%fused_computation.2 | convolution fusion | flops 3682271232 | bytes 9928704 | tf_op jit(solution)/shard_map/dot_general | solution.py:17
  461.8 10.3 %convolution_convert_fusion.2 = bf16[768,3072]{1,0:T(8,128)(2,1)} fusion(bf16[1040,768]{1,0:T(8,128)(2,1)} %constant_dynamic-update-slice_fusion.20, bf16[1040,3072]{1,0:T(8,128)(2,1)} %constant_dynamic-update-slice_fusion.5), kind=kOutput, calls=%fused_computation.4 | convolution fusion | flops 4909694976 | bytes 12705792 | tf_op jit(solution)/shard_map/dot_general | solution.py:17
  480.1 8.0 convolution_convert_fusion.1
  490.0 3.6 fusion.10
  500.2 21.4 %all-reduce.7.cloned.1.call-done = f32[128,128]{1,0:T(8,128)} async-done(((f32[128,128]{1,0:T(8,128)}), f32[128,128]{1,0:T(8,128)}) %all-reduce.7.cloned.1.call-update) | async-done | bytes 65552
  524.1 61.1 %reduce-scatter.7.cloned.1.call-done = bf16[48,768]{1,0:T(8,128)(2,1)} async-done(((bf16[768,768]{1,0:T(8,128)(2,1)}), bf16[48,768]{1,0:T(8,128)(2,1)}) %reduce-scatter.7.cloned.1.call-update) | async-done | bytes 73744 | tf_op jit(solution)/shard_map/reduce_scatter | solution.py:246
  586.7 69.9 %reduce-scatter.5.cloned.1.call-done = bf16[48,2304]{1,0:T(8,128)(2,1)} async-done(((bf16[768,2304]{1,0:T(8,128)(2,1)}), bf16[48,2304]{1,0:T(8,128)(2,1)}) %reduce-scatter.5.cloned.1.call-update) | async-done | bytes 221200 | tf_op jit(solution)/shard_map/reduce_scatter | solution.py:246
  658.3 77.1 %reduce-scatter.9.cloned.1.call-done = bf16[48,3072]{1,0:T(8,128)(2,1)} async-done(((bf16[768,3072]{1,0:T(8,128)(2,1)}), bf16[48,3072]{1,0:T(8,128)(2,1)}) %reduce-scatter.9.cloned.1.call-update) | async-done | bytes 294928 | tf_op jit(solution)/shard_map/reduce_scatter | solution.py:246
  737.3 76.7 %reduce-scatter.11.cloned.1.call-done = bf16[192,768]{1,0:T(8,128)(2,1)} async-done(((bf16[3072,768]{1,0:T(8,128)(2,1)}), bf16[192,768]{1,0:T(8,128)(2,1)}) %reduce-scatter.11.cloned.1.call-update) | async-done | bytes 294928 | tf_op jit(solution)/shard_map/reduce_scatter | solution.py:246
  (603 shorter events, 130.5 us)
Async XLA Ops:
  7.2 32.3 %copy-start.85 = (bf16[4,197,768]{2,0,1:T(4,128)(2,1)S(1)}, bf16[4,197,768]{2,0,1:T(4,128)(2,1)}, u32[]{:S(2)}) copy-start(bf16[4,197,768]{2,0,1:T(4,128)(2,1)} %param.15) | copy-start | bytes 3631108
  7.2 32.7 %copy-start.162 = (s32[4]{0:T(128)S(1)}, s32[4]{0:T(128)}, u32[]{:S(2)}) copy-start(s32[4]{0:T(128)} %param.17) | copy-start | bytes 52
  7.2 53.1 %all-gather.9.cloned.1.call-start = ((), (), s32[]{:S(2)}) async-start(), calls=%async_computation.8 | async-start | bytes 3760128 | tf_op jit(solution)/shard_map/all_gather | solution.py:199
  7.9 92.0 %all-gather.11.cloned.1.call-start = ((), (), s32[]{:S(2)}) async-start(), calls=%async_computation.9 | async-start | bytes 1253376 | tf_op jit(solution)/shard_map/all_gather | solution.py:199
  8.7 145.8 %all-gather.13.cloned.1.call-start = ((), (), s32[]{:S(2)}) async-start(), calls=%async_computation.10 | async-start | bytes 5013504 | tf_op jit(solution)/shard_map/all_gather | solution.py:199
  9.4 199.0 %all-gather.15.cloned.1.call-start = ((), (), s32[]{:S(2)}) async-start(), calls=%async_computation.11 | async-start | bytes 5013504 | tf_op jit(solution)/shard_map/all_gather | solution.py:199
  10.0 511.6 %all-reduce.7.cloned.1.call-start = ((), (), s32[]{:S(2)}) async-start(), calls=%async_computation.12 | async-start | bytes 131072
  39.7 183.9 %copy-start.17 = (bf16[4,197,768]{2,1,0:T(8,128)(2,1)}, bf16[4,197,768]{2,1,0:T(8,128)(2,1)S(1)}, u32[]{:S(2)}) copy-start(bf16[4,197,768]{2,1,0:T(8,128)(2,1)S(1)} %copy.33) | copy-start | bytes 3631108
  39.7 213.4 %copy-start.106 = (f32[3072]{0:T(1024)}, f32[3072]{0:T(1024)S(1)}, u32[]{:S(2)}) copy-start(f32[3072]{0:T(1024)S(1)} %add.502) | copy-start | bytes 36868
  40.0 239.7 %copy-start.95 = (f32[768]{0:T(1024)}, f32[768]{0:T(1024)S(1)}, u32[]{:S(2)}) copy-start(f32[768]{0:T(1024)S(1)} %add.508) | copy-start | bytes 9220
  40.7 206.7 %copy-start.109 = (f32[2304]{0:T(1024)}, f32[2304]{0:T(1024)S(1)}, u32[]{:S(2)}) copy-start(f32[2304]{0:T(1024)S(1)} %get-tuple-element.174) | copy-start | bytes 27652
  40.7 206.7 %copy-start.110 = (f32[2304]{0:T(1024)}, f32[2304]{0:T(1024)S(1)}, u32[]{:S(2)}) copy-start(f32[2304]{0:T(1024)S(1)} %get-tuple-element.175) | copy-start | bytes 27652
  40.8 22.5 %copy-start.138 = (f32[208]{0:T(256)}, f32[208]{0:T(256)S(1)}, u32[]{:S(2)}) copy-start(f32[208]{0:T(256)S(1)} %broadcast_multiply_fusion.30) | copy-start | bytes 2500
  41.0 22.3 %copy-start.126 = (f32[208]{0:T(256)}, f32[208]{0:T(256)S(1)}, u32[]{:S(2)}) copy-start(f32[208]{0:T(256)S(1)} %add_rsqrt_fusion.9) | copy-start | bytes 2500
  101.7 106.7 %copy-start.54 = (f32[208,768]{1,0:T(8,128)}, f32[208,768]{1,0:T(8,128)S(1)}, u32[]{:S(2)}) copy-start(f32[208,768]{1,0:T(8,128)S(1)} %get-tuple-element.156) | copy-start | bytes 1916932
  101.7 58.9 %copy-start.124 = (f32[208]{0:T(256)}, f32[208]{0:T(256)S(1)}, u32[]{:S(2)}) copy-start(f32[208]{0:T(256)S(1)} %broadcast_multiply_fusion.29) | copy-start | bytes 2500
  102.0 58.7 %copy-start.146 = (f32[208]{0:T(256)}, f32[208]{0:T(256)S(1)}, u32[]{:S(2)}) copy-start(f32[208]{0:T(256)S(1)} %add_rsqrt_fusion.8) | copy-start | bytes 2500
  212.9 14.5 %copy-start.88 = (bf16[208,768]{1,0:T(8,128)(2,1)}, bf16[208,768]{1,0:T(8,128)(2,1)S(1)}, u32[]{:S(2)}) copy-start(bf16[208,768]{1,0:T(8,128)(2,1)S(1)} %fusion.185) | copy-start | bytes 958468
  213.0 10.6 %collective-permute-start = (bf16[208,768]{1,0:T(8,128)(2,1)S(1)}, bf16[208,768]{1,0:T(8,128)(2,1)S(1)}, u32[]{:S(2)}, u32[]{:S(2)}) collective-permute-start(bf16[208,768]{1,0:T(8,128)(2,1)S(1)} %fusion.185), channel_id=1, source_target_pairs={{0,16},{1,17},{2,18},{3,19},{4,20},{5,21},{6,22},{7,23},{8,24},{9,... | collective-permute-start | bytes 958472 | tf_op jit(solution)/shard_map/ppermute | solution.py:218
  235.1 15.5 %copy-start.90 = (bf16[208,768]{1,0:T(8,128)(2,1)}, bf16[208,768]{1,0:T(8,128)(2,1)S(1)}, u32[]{:S(2)}) copy-start(bf16[208,768]{1,0:T(8,128)(2,1)S(1)} %fusion.182) | copy-start | bytes 958468
  235.1 10.8 %collective-permute-start.1 = (bf16[208,768]{1,0:T(8,128)(2,1)S(1)}, bf16[208,768]{1,0:T(8,128)(2,1)S(1)}, u32[]{:S(2)}, u32[]{:S(2)}) collective-permute-start(bf16[208,768]{1,0:T(8,128)(2,1)S(1)} %fusion.182), channel_id=1, source_target_pairs={{0,16},{1,17},{2,18},{3,19},{4,20},{5,21},{6,22},{7,23},{8,24},{9,... | collective-permute-start | bytes 958472 | tf_op jit(solution)/shard_map/ppermute | solution.py:218
  258.1 15.2 %copy-start.92 = (bf16[208,768]{1,0:T(8,128)(2,1)}, bf16[208,768]{1,0:T(8,128)(2,1)S(1)}, u32[]{:S(2)}) copy-start(bf16[208,768]{1,0:T(8,128)(2,1)S(1)} %fusion.179) | copy-start | bytes 958468
  258.1 9.9 %collective-permute-start.2 = (bf16[208,768]{1,0:T(8,128)(2,1)S(1)}, bf16[208,768]{1,0:T(8,128)(2,1)S(1)}, u32[]{:S(2)}, u32[]{:S(2)}) collective-permute-start(bf16[208,768]{1,0:T(8,128)(2,1)S(1)} %fusion.179), channel_id=1, source_target_pairs={{0,16},{1,17},{2,18},{3,19},{4,20},{5,21},{6,22},{7,23},{8,24},{9,... | collective-permute-start | bytes 958472 | tf_op jit(solution)/shard_map/ppermute | solution.py:218
  281.7 9.2 %collective-permute-start.3 = (bf16[208,768]{1,0:T(8,128)(2,1)}, bf16[208,768]{1,0:T(8,128)(2,1)S(1)}, u32[]{:S(2)}, u32[]{:S(2)}) collective-permute-start(bf16[208,768]{1,0:T(8,128)(2,1)} %fusion.176), channel_id=1, source_target_pairs={{0,16},{1,17},{2,18},{3,19},{4,20},{5,21},{6,22},{7,23},{8,24},{9,... | collective-permute-start | bytes 958472 | tf_op jit(solution)/shard_map/ppermute | solution.py:218
  292.2 21.8 %copy-start.50 = (bf16[208,768]{1,0:T(8,128)(2,1)}, bf16[208,768]{1,0:T(8,128)(2,1)S(1)}, u32[]{:S(2)}) copy-start(bf16[208,768]{1,0:T(8,128)(2,1)S(1)} %get-tuple-element.108) | copy-start | bytes 958468
  292.5 21.5 %copy-start.122 = (f32[208]{0:T(256)}, f32[208]{0:T(256)S(1)}, u32[]{:S(2)}) copy-start(f32[208]{0:T(256)S(1)} %add_rsqrt_fusion.1) | copy-start | bytes 2500
  315.0 9.2 %collective-permute-start.4 = (bf16[208,768]{1,0:T(8,128)(2,1)}, bf16[208,768]{1,0:T(8,128)(2,1)}, u32[]{:S(2)}, u32[]{:S(2)}) collective-permute-start(bf16[208,768]{1,0:T(8,128)(2,1)} %fusion.231), channel_id=1, source_target_pairs={{16,0},{17,1},{18,2},{19,3},{20,4},{21,5},{22,6},{23,7},{24,8},{25... | collective-permute-start | bytes 958472 | tf_op jit(solution)/shard_map/ppermute | solution.py:236
  317.2 18.1 %copy-start.140 = (f32[208]{0:T(256)}, f32[208]{0:T(256)S(1)}, u32[]{:S(2)}) copy-start(f32[208]{0:T(256)S(1)} %fusion.312) | copy-start | bytes 2500
  317.2 40.6 %copy-start.142 = (f32[208]{0:T(256)}, f32[208]{0:T(256)S(1)}, u32[]{:S(2)}) copy-start(f32[208]{0:T(256)S(1)} %fusion.311) | copy-start | bytes 2500
  325.3 10.0 %copy-start.56 = (bf16[208,768]{1,0:T(8,128)(2,1)}, bf16[208,768]{1,0:T(8,128)(2,1)S(1)}, u32[]{:S(2)}) copy-start(bf16[208,768]{1,0:T(8,128)(2,1)S(1)} %fusion.284) | copy-start | bytes 958468
  329.9 23.6 %slice-start.8 = ((s8[4718592]{0:T(1024)(128)(4,1)}), s8[4194304]{0:T(1024)(128)(4,1)S(1)}, s32[]{:S(2)}) async-start(s8[4718592]{0:T(1024)(128)(4,1)} %bitcast.337), calls=%async_computation.21 | async-start | bytes 8388608
  337.1 16.4 %slice-start.9 = ((s8[4718592]{0:T(1024)(128)(4,1)}), s8[524288]{0:T(1024)(128)(4,1)S(1)}, s32[]{:S(2)}) async-start(s8[4718592]{0:T(1024)(128)(4,1)} %bitcast.337), calls=%async_computation.22 | async-start | bytes 1048576
  344.0 9.5 %copy-start.20 = (bf16[4,197,768]{2,1,0:T(8,128)(2,1)S(1)}, bf16[4,197,768]{2,1,0:T(8,128)(2,1)}, u32[]{:S(2)}) copy-start(bf16[4,197,768]{2,1,0:T(8,128)(2,1)} %copy.34) | copy-start | bytes 3631108
  344.3 9.2 %copy-start.79 = (bf16[208,768]{1,0:T(8,128)(2,1)}, bf16[208,768]{1,0:T(8,128)(2,1)S(1)}, u32[]{:S(2)}) copy-start(bf16[208,768]{1,0:T(8,128)(2,1)S(1)} %fusion.240) | copy-start | bytes 958468
  344.3 9.3 %copy-start.166 = (bf16[208,3072]{1,0:T(8,128)(2,1)S(1)}, bf16[208,3072]{1,0:T(8,128)(2,1)}, u32[]{:S(2)}) copy-start(bf16[208,3072]{1,0:T(8,128)(2,1)} %get-tuple-element.31) | copy-start | bytes 3833860
  344.3 9.1 %collective-permute-start.5 = (bf16[208,768]{1,0:T(8,128)(2,1)S(1)}, bf16[208,768]{1,0:T(8,128)(2,1)S(1)}, u32[]{:S(2)}, u32[]{:S(2)}) collective-permute-start(bf16[208,768]{1,0:T(8,128)(2,1)S(1)} %fusion.240), channel_id=1, source_target_pairs={{16,0},{17,1},{18,2},{19,3},{20,4},{21,5},{22,6},{23,7},{24,8},{25... | collective-permute-start | bytes 958472 | tf_op jit(solution)/shard_map/ppermute | solution.py:236
  346.2 33.1 %copy-start.144 = (f32[208]{0:T(256)}, f32[208]{0:T(256)S(1)}, u32[]{:S(2)}) copy-start(f32[208]{0:T(256)S(1)} %fusion.310) | copy-start | bytes 2500
  346.2 9.1 %slice-start.18 = ((s8[4718592]{0:T(1024)(128)(4,1)}), s8[4194304]{0:T(1024)(128)(4,1)S(1)}, s32[]{:S(2)}) async-start(s8[4718592]{0:T(1024)(128)(4,1)} %bitcast.360), calls=%async_computation.31 | async-start | bytes 8388608
  366.1 9.0 %copy-start.81 = (bf16[208,768]{1,0:T(8,128)(2,1)}, bf16[208,768]{1,0:T(8,128)(2,1)S(1)}, u32[]{:S(2)}) copy-start(bf16[208,768]{1,0:T(8,128)(2,1)S(1)} %fusion.249) | copy-start | bytes 958468
  366.1 9.1 %copy-start.165 = (bf16[208,3072]{1,0:T(8,128)(2,1)S(1)}, bf16[208,3072]{1,0:T(8,128)(2,1)}, u32[]{:S(2)}) copy-start(bf16[208,3072]{1,0:T(8,128)(2,1)} %get-tuple-element.32) | copy-start | bytes 3833860
  366.1 9.0 %collective-permute-start.6 = (bf16[208,768]{1,0:T(8,128)(2,1)S(1)}, bf16[208,768]{1,0:T(8,128)(2,1)S(1)}, u32[]{:S(2)}, u32[]{:S(2)}) collective-permute-start(bf16[208,768]{1,0:T(8,128)(2,1)S(1)} %fusion.249), channel_id=1, source_target_pairs={{16,0},{17,1},{18,2},{19,3},{20,4},{21,5},{22,6},{23,7},{24,8},{25... | collective-permute-start | bytes 958472 | tf_op jit(solution)/shard_map/ppermute | solution.py:236
  386.9 9.9 %copy-start.164 = (bf16[208,3072]{1,0:T(8,128)(2,1)S(1)}, bf16[208,3072]{1,0:T(8,128)(2,1)}, u32[]{:S(2)}) copy-start(bf16[208,3072]{1,0:T(8,128)(2,1)} %get-tuple-element.33) | copy-start | bytes 3833860
  386.9 9.0 %collective-permute-start.7 = (bf16[208,768]{1,0:T(8,128)(2,1)S(1)}, bf16[208,768]{1,0:T(8,128)(2,1)S(1)}, u32[]{:S(2)}, u32[]{:S(2)}) collective-permute-start(bf16[208,768]{1,0:T(8,128)(2,1)S(1)} %fusion.258), channel_id=1, source_target_pairs={{16,0},{17,1},{18,2},{19,3},{20,4},{21,5},{22,6},{23,7},{24,8},{25... | collective-permute-start | bytes 958472 | tf_op jit(solution)/shard_map/ppermute | solution.py:236
  388.6 9.8 %copy-start.94 = (bf16[1040,768]{1,0:T(8,128)(2,1)}, bf16[1040,768]{1,0:T(8,128)(2,1)S(1)}, u32[]{:S(2)}) copy-start(bf16[1040,768]{1,0:T(8,128)(2,1)S(1)} %constant_dynamic-update-slice_fusion.15) | copy-start | bytes 4792324
  439.3 145.9 %reduce-scatter.7.cloned.1.call-start = ((), (), s32[]{:S(2)}) async-start(), calls=%async_computation.5 | async-start | bytes 1253376 | tf_op jit(solution)/shard_map/reduce_scatter | solution.py:246
  443.7 212.9 %reduce-scatter.5.cloned.1.call-start = ((), (), s32[]{:S(2)}) async-start(), calls=%async_computation.4 | async-start | bytes 3760128 | tf_op jit(solution)/shard_map/reduce_scatter | solution.py:246
  457.1 278.3 %reduce-scatter.9.cloned.1.call-start = ((), (), s32[]{:S(2)}) async-start(), calls=%async_computation.6 | async-start | bytes 5013504 | tf_op jit(solution)/shard_map/reduce_scatter | solution.py:246
  472.1 341.8 %reduce-scatter.11.cloned.1.call-start = ((), (), s32[]{:S(2)}) async-start(), calls=%async_computation.7 | async-start | bytes 5013504 | tf_op jit(solution)/shard_map/reduce_scatter | solution.py:246
  (156 other events, 536.2 us)
Sparse Core Ops, SparseCore 0:
  10.3 49.9 all-gather.8
  62.6 37.3 all-gather.10
  102.2 52.1 all-gather.12
  156.6 51.7 all-gather.14
  439.4 82.1 all-reduce.6
  525.5 59.6 reduce-scatter.6
  589.5 66.9 reduce-scatter.4
  660.9 74.4 reduce-scatter.8
  739.3 74.6 reduce-scatter.10

commit v2 on v1

--- a/solution.py
+++ b/solution.py
@@ -160,6 +160,10 @@
     return middle_grad + part, sums, (down_grad, up_grad, out_grad, joint_grad)
 
 
+def columns_cut(member, width):
+    return [member[:, at : at + width] for at in range(0, member.shape[1], width)]
+
+
 def body(
     images,
     cotangent,
@@ -186,19 +190,29 @@
 
     shards = (normgain, normbias, qvbias, outbias, mlpgain, mlpbias, upbias, downbias)
     lengths = [member.shape[1] for member in shards]
-    packed = jnp.concatenate([member[0].astype(F32) for member in shards])
-    room = -(-packed.shape[0] // 1024) * 1024
-    packed = jnp.pad(packed, (0, room - packed.shape[0])).reshape(room // 128, 128)
-    packed = lax.all_gather(packed, "fsdp", axis=0, tiled=True).reshape(peers, room)
+    joined_small = jnp.concatenate([member[0] for member in shards])
+    room = -(-joined_small.shape[0] // (16 * width)) * 16
+    matrices = (qkvweight, outweight, upweight, downweight)
+    shapes = [member.shape[1:] for member in matrices]
+    pieces = [cut for member in matrices for cut in columns_cut(member[0], width)]
+    pieces.append(
+        jnp.pad(joined_small, (0, room * width - joined_small.shape[0])).reshape(room, width)
+    )
+    gathered = lax.all_gather(jnp.concatenate(pieces, axis=0), "fsdp", axis=0)
+    large = []
+    at = 0
+    for shape in shapes:
+        cuts = []
+        for _ in range(shape[1] // width):
+            cuts.append(gathered[:, at : at + shape[0]].reshape(peers * shape[0], width))
+            at += shape[0]
+        large.append(jnp.concatenate(cuts, axis=1))
+    flat = gathered[:, at:].reshape(peers, room * width).astype(F32)
     small = []
     at = 0
     for length in lengths:
-        small.append(packed[:, at : at + length].reshape(-1))
+        small.append(flat[:, at : at + length].reshape(-1))
         at += length
-    large = tuple(
-        lax.all_gather(member[0], "fsdp", axis=0, tiled=True)
-        for member in (qkvweight, outweight, upweight, downweight)
-    )
     images = jnp.pad(images, padding)
     cotangent = jnp.pad(cotangent, padding)
 
@@ -241,14 +255,12 @@
     down_grad, up_grad, out_grad, joint_grad = (joined(m) for m in zip(*grads))
     _, normed, _, mixed, _, normed_mlp, hidden, _ = zip(*kept)
 
-    def spread(left, right):
-        total = dot(joined(left), right, 0, 0).astype(BF16)
-        return lax.psum_scatter(total, "fsdp", scatter_dimension=0, tiled=True).astype(F32)[None]
-
-    down_sum = spread(hidden, down_grad)
-    up_sum = spread(normed_mlp, up_grad)
-    out_sum = spread(mixed, out_grad)
-    qkv_sum = spread(normed, joint_grad)
+    totals = (
+        dot(joined(normed), joint_grad, 0, 0).astype(BF16),
+        dot(joined(mixed), out_grad, 0, 0).astype(BF16),
+        dot(joined(normed_mlp), up_grad, 0, 0).astype(BF16),
+        dot(joined(hidden), down_grad, 0, 0).astype(BF16),
+    )
 
     def rows_sum(member):
         return jnp.sum(member.astype(F32), axis=0)
@@ -265,13 +277,27 @@
         rows_sum(down_grad),
     )
     packed = jnp.concatenate([vector.reshape(peers, -1) for vector in vectors], axis=1)
-    packed = jnp.pad(packed, ((0, 0), (0, room - packed.shape[1])))
-    packed = packed.reshape(peers * room // 128, 128)
-    packed = lax.psum_scatter(packed, "fsdp", scatter_dimension=0, tiled=True).reshape(1, room)
+    packed = jnp.pad(packed.astype(BF16), ((0, 0), (0, room * width - packed.shape[1])))
+    pieces = [
+        cut.reshape(peers, -1, width) for total in totals for cut in columns_cut(total, width)
+    ]
+    pieces.append(packed.reshape(peers, room, width))
+    stacked = jnp.concatenate(pieces, axis=1).reshape(-1, width)
+    summed = lax.psum_scatter(stacked, "fsdp", scatter_dimension=0, tiled=True)
+    wholes = []
+    at = 0
+    for shape in shapes:
+        cuts = []
+        for _ in range(shape[1] // width):
+            cuts.append(summed[at : at + shape[0]])
+            at += shape[0]
+        wholes.append(jnp.concatenate(cuts, axis=1).astype(F32)[None])
+    qkv_sum, out_sum, up_sum, down_sum = wholes
+    flat = summed[at:].reshape(1, room * width).astype(F32)
     outs = []
     at = 0
     for length in lengths:
-        outs.append(packed[:, at : at + length])
+        outs.append(flat[:, at : at + length])
         at += length
 
     def by_batch(members):

time: 829 us -> 580 us (0.70)
  waiting for transfers between devices: 507 us -> 286 us
  local copies, waits for them, and re-layouts: 39.1 us -> 72.6 us
  matrix products: 123 us -> 92.6 us
  blocking collectives: 23.4 us -> 0 us
    reduce_scatter x4 -> x1, waiting for transfers between devices: 285 us -> 135 us  [body(): summed = lax.psum_scatter(stacked, 'fsdp', scatter_dimension=0, tiled=True)]
    all_gather x4 -> x1, waiting for transfers between devices: 154 us -> 105 us  [body(): gathered = lax.all_gather(jnp.concatenate(pieces, axis=0), 'fsdp', axis=0)]
    dot_general x44, matrix products: 123 us -> 92.6 us  [dot(): return lax.dot_general(left, right, dims, preferred_element_type=F32)]
    unnamed x10 -> x2, waiting for transfers between devices: 24 us -> 0.03 us
    all_gather x1 -> x0, blocking collectives: 23.4 us -> none  [body(): lax.all_gather(packed, 'fsdp', axis=0, tiled=True).reshape(peers, room)]
    unnamed x396 -> x189, local copies, waits for them, and re-layouts: 27.4 us -> 42.6 us
    slice x5 -> x9, local copies, waits for them, and re-layouts: 1.96 us -> 14.2 us  [the longest x2 11.7 us: body(): cuts.append(gathered[:, at:at + shape[0]].reshape(peers * shape[0], width))]
    reduce_sum x4 -> x24, other arithmetic: 10.6 us -> 16.9 us  [rows_sum(): return jnp.sum(member.astype(F32), axis=0)]
  transfers between devices with their start and end apart: 17 -> 10, of which waited for: 17 -> 10; matrix products, arithmetic and copies ran while one was open for 10% -> 4% of each run, Pallas kernels for 0% -> 0%
where the time goes in v2:
time: 580 us; the launch traced here: 572 us
  waiting for transfers between devices  286 us (49%)
  matrix products  92.6 us (16%)
  local copies, waits for them, and re-layouts  72.6 us (13%)
  other arithmetic  42.5 us (7%)
  Pallas kernels  32.8 us (6%)
  starting transfers between devices  24.4 us (4%)
  between operations  21.5 us (4%)
    reduce_scatter x1, waiting for transfers between devices, body(): summed = lax.psum_scatter(stacked, 'fsdp', scatter_dimension=0, tiled=True)  135 us
    all_gather x1, waiting for transfers between devices, body(): gathered = lax.all_gather(jnp.concatenate(pieces, axis=0), 'fsdp', axis=0)  105 us
    dot_general x44, matrix products, dot(): return lax.dot_general(left, right, dims, preferred_element_type=F32)  92.6 us
    unnamed x189, local copies, waits for them, and re-layouts  42.6 us
    ppermute x4, waiting for transfers between devices, body(): incoming = lax.ppermute(entries[tick], 'section', [(1, 0)])  26.4 us
    pallas_call x5, Pallas kernels, attend_back(): pl.pallas_call(lambda *refs: attend_back_kernel(tokens, width, *refs), ou...  24.4 us
    ppermute x4, waiting for transfers between devices, body(): incoming = lax.ppermute(leaving_low, 'section', [(0, 1)])  19.2 us
    ppermute x4, starting transfers between devices, body(): incoming = lax.ppermute(leaving_low, 'section', [(0, 1)])  17.5 us
  transfers between devices with their start and end apart: 10, of which 10 were waited for; matrix products, arithmetic and copies ran while one was open for 4% of the time, Pallas kernels for 0%

profile of v2, /device:TPU:0, one launch (start us, length us, event | category | flops | bytes accessed | tf_op | source)
XLA Modules:
  0.0 572.3 jit_solution(14720528222942165850)
XLA Ops:
  7.9 4.8 concatenate.93
  29.1 2.9 copy.30
  32.4 105.3 %all-gather.3.cloned.1.call-done = bf16[9472,768]{1,0:T(8,128)(2,1)} async-done(((bf16[592,768]{1,0:T(8,128)(2,1)}), bf16[9472,768]{1,0:T(8,128)(2,1)}) %all-gather.3.cloned.1.call-update) | async-done | bytes 14549008 | tf_op jit(solution)/shard_map/all_gather | solution.py:201
  139.5 4.9 slice.381
  144.4 6.7 %fusion.195 = (bf16[16,48,768]{2,1,0:T(8,128)(2,1)S(1)}, bf16[16,48,768]{2,1,0:T(8,128)(2,1)}, bf16[16,48,768]{2,1,0:T(8,128)(2,1)}, bf16[16,48,768]{2,1,0:T(8,1...) fusion(bf16[16,592,768]{2,1,0:T(8,128)(2,1)} %bitcast.247), kind=kLoop, calls=%fused_computation.440 | loop fusion | bytes 18874368 | tf_op jit(solution)/shard_map/slice | solution.py:207
  152.1 3.0 fusion.10.refs_0_
  159.7 3.8 fusion.19
  163.6 1.8 fusion.53
  165.5 3.9 collective-permute-start
  170.5 5.8 %collective-permute-done = bf16[208,768]{1,0:T(8,128)(2,1)S(1)} collective-permute-done((bf16[208,768]{1,0:T(8,128)(2,1)S(1)}, bf16[208,768]{1,0:T(8,128)(2,1)S(1)}, u32[]{:S(2)}, u32[]{:S(2)}) %collective-permute-start) | collective-permute-done | bytes 319520 | tf_op jit(solution)/shard_map/ppermute | solution.py:232
  180.5 3.8 fusion.24
  185.7 4.4 collective-permute-start.1
  191.3 5.2 collective-permute-done.1
  200.7 3.8 fusion.29
  205.9 4.8 collective-permute-start.2
  211.8 3.9 collective-permute-done.2
  219.7 3.8 fusion.34
  224.7 4.4 collective-permute-start.3
  229.3 4.3 collective-permute-done.3
  237.6 3.2 fusion.39
  242.4 1.9 multiply_reduce_fusion.4
  246.0 4.9 attend_back.5
  254.6 7.1 %collective-permute-done.4 = bf16[208,768]{1,0:T(8,128)(2,1)S(1)} collective-permute-done((bf16[208,768]{1,0:T(8,128)(2,1)S(1)}, bf16[208,768]{1,0:T(8,128)(2,1)S(1)}, u32[]{:S(2)}, u32[]{:S(2)}) %collective-permute-start.4) | collective-permute-done | bytes 319520 | tf_op jit(solution)/shard_map/ppermute | solution.py:250
  263.5 1.9 multiply_reduce_fusion.3
  266.3 4.9 attend_back.6
  275.8 6.2 %collective-permute-done.5 = bf16[208,768]{1,0:T(8,128)(2,1)S(1)} collective-permute-done((bf16[208,768]{1,0:T(8,128)(2,1)S(1)}, bf16[208,768]{1,0:T(8,128)(2,1)S(1)}, u32[]{:S(2)}, u32[]{:S(2)}) %collective-permute-start.5) | collective-permute-done | bytes 319520 | tf_op jit(solution)/shard_map/ppermute | solution.py:250
  283.9 1.9 multiply_reduce_fusion.2
  286.7 4.9 attend_back.7
  293.4 1.9 collective-permute-start.6
  295.6 6.8 %collective-permute-done.6 = bf16[208,768]{1,0:T(8,128)(2,1)S(1)} collective-permute-done((bf16[208,768]{1,0:T(8,128)(2,1)S(1)}, bf16[208,768]{1,0:T(8,128)(2,1)S(1)}, u32[]{:S(2)}, u32[]{:S(2)}) %collective-permute-start.6) | collective-permute-done | bytes 319520 | tf_op jit(solution)/shard_map/ppermute | solution.py:250
  304.3 1.9 multiply_reduce_fusion.1
  308.0 4.9 attend_back.8
  317.4 6.3 %collective-permute-done.7 = bf16[208,768]{1,0:T(8,128)(2,1)S(1)} collective-permute-done((bf16[208,768]{1,0:T(8,128)(2,1)S(1)}, bf16[208,768]{1,0:T(8,128)(2,1)S(1)}, u32[]{:S(2)}, u32[]{:S(2)}) %collective-permute-start.7) | collective-permute-done | bytes 319520 | tf_op jit(solution)/shard_map/ppermute | solution.py:250
  325.5 1.9 multiply_reduce_fusion
  330.1 4.9 attend_back.9
  335.0 2.9 multiply_reduce_fusion.5
  343.7 2.0 constant_dynamic-update-slice_fusion.27
  345.6 1.9 constant_dynamic-update-slice_fusion.26
  347.5 2.0 constant_dynamic-update-slice_fusion.25
  349.5 1.8 constant_dynamic-update-slice_fusion.24
  353.7 2.3 fusion.203
  360.6 7.9 %convolution_convert_fusion = bf16[768,2304]{1,0:T(8,128)(2,1)S(1)} fusion(bf16[1040,768]{1,0:T(8,128)(2,1)} %copy-done.55, bf16[1040,2304]{1,0:T(8,128)(2,1)} %get-tuple-element.162), kind=kOutput, calls=%fused_computation | convolution fusion | flops 3682271232 | bytes 9928704 | tf_op jit(solution)/shard_map/dot_general | solution.py:17
  378.4 8.9 %convolution_convert_fusion.2 = bf16[768,3072]{1,0:T(8,128)(2,1)S(1)} fusion(bf16[1040,768]{1,0:T(8,128)(2,1)} %get-tuple-element.179, bf16[1040,3072]{1,0:T(8,128)(2,1)} %get-tuple-element.149), kind=kOutput, calls=%fused_computation.2 | convolution fusion | flops 4909694976 | bytes 12705792 | tf_op jit(solution)/shard_map/dot_general | solution.py:17
  392.3 7.1 %convolution_convert_fusion.1 = bf16[3072,768]{1,0:T(8,128)(2,1)S(1)} fusion(bf16[1040,3072]{1,0:T(8,128)(2,1)S(1)} %bitcast.302, bf16[1040,768]{1,0:T(8,128)(2,1)S(1)} %copy-done.62), kind=kOutput, calls=%fused_computation.1 | convolution fusion | flops 4909694976 | bytes 12705792 | tf_op jit(solution)/shard_map/dot_general | solution.py:17
  407.3 2.6 constant_dynamic-update-slice_fusion.49
  412.0 4.2 fusion.218
  422.0 135.1 %reduce-scatter.2.cloned.1.call-done = bf16[592,768]{1,0:T(8,128)(2,1)} async-done(((bf16[9472,768]{1,0:T(8,128)(2,1)}), bf16[592,768]{1,0:T(8,128)(2,1)}) %reduce-scatter.2.cloned.1.call-update) | async-done | bytes 909328 | tf_op jit(solution)/shard_map/reduce_scatter | solution.py:286
  559.7 1.8 slice_bitcast_fusion.4
  (383 shorter events, 123.7 us)
Async XLA Ops:
  7.2 14.7 %copy-start.69 = (s32[4]{0:T(128)S(1)}, s32[4]{0:T(128)}, u32[]{:S(2)}) copy-start(s32[4]{0:T(128)} %param.17) | copy-start | bytes 52
  7.2 130.5 %all-gather.3.cloned.1.call-start = ((), (), s32[]{:S(2)}) async-start(), calls=%async_computation.2 | async-start | bytes 15458304 | tf_op jit(solution)/shard_map/all_gather | solution.py:201
  21.8 535.3 %reduce-scatter.2.cloned.1.call-start = ((), (), s32[]{:S(2)}) async-start(), calls=%async_computation.1 | async-start | bytes 15458304 | tf_op jit(solution)/shard_map/reduce_scatter | solution.py:286
  29.1 204.5 %copy-start.3 = (bf16[4,197,768]{2,1,0:T(8,128)(2,1)}, bf16[4,197,768]{2,1,0:T(8,128)(2,1)S(1)}, u32[]{:S(2)}) copy-start(bf16[4,197,768]{2,1,0:T(8,128)(2,1)S(1)} %copy.29) | copy-start | bytes 3631108
  32.4 302.5 %copy-start.65 = (f32[208]{0:T(256)}, f32[208]{0:T(256)S(1)}, u32[]{:S(2)}) copy-start(f32[208]{0:T(256)S(1)} %add_rsqrt_fusion.9) | copy-start | bytes 2500
  151.2 135.0 %copy-start.1 = (bf16[16,48,768]{2,1,0:T(8,128)(2,1)}, bf16[16,48,768]{2,1,0:T(8,128)(2,1)S(1)}, u32[]{:S(2)}) copy-start(bf16[16,48,768]{2,1,0:T(8,128)(2,1)S(1)} %get-tuple-element.115) | copy-start | bytes 3538948
  151.5 72.0 %copy-start.63 = (f32[768]{0:T(1024)}, f32[768]{0:T(1024)S(1)}, u32[]{:S(2)}) copy-start(f32[768]{0:T(1024)S(1)} %add.500) | copy-start | bytes 9220
  159.1 4.5 slice-start
  165.4 11.1 %copy-start.47 = (bf16[208,768]{1,0:T(8,128)(2,1)}, bf16[208,768]{1,0:T(8,128)(2,1)S(1)}, u32[]{:S(2)}) copy-start(bf16[208,768]{1,0:T(8,128)(2,1)S(1)} %fusion.53) | copy-start | bytes 958468
  165.4 11.3 %copy-start.41 = (bf16[16,48,768]{2,1,0:T(8,128)(2,1)S(1)}, bf16[16,48,768]{2,1,0:T(8,128)(2,1)}, u32[]{:S(2)}) copy-start(bf16[16,48,768]{2,1,0:T(8,128)(2,1)} %get-tuple-element.120) | copy-start | bytes 3538948
  165.4 11.3 %copy-start.42 = (bf16[16,48,768]{2,1,0:T(8,128)(2,1)S(1)}, bf16[16,48,768]{2,1,0:T(8,128)(2,1)}, u32[]{:S(2)}) copy-start(bf16[16,48,768]{2,1,0:T(8,128)(2,1)} %get-tuple-element.121) | copy-start | bytes 3538948
  165.4 11.3 %copy-start.43 = (bf16[16,48,768]{2,1,0:T(8,128)(2,1)S(1)}, bf16[16,48,768]{2,1,0:T(8,128)(2,1)}, u32[]{:S(2)}) copy-start(bf16[16,48,768]{2,1,0:T(8,128)(2,1)} %get-tuple-element.122) | copy-start | bytes 3538948
  165.5 10.9 %collective-permute-start = (bf16[208,768]{1,0:T(8,128)(2,1)S(1)}, bf16[208,768]{1,0:T(8,128)(2,1)S(1)}, u32[]{:S(2)}, u32[]{:S(2)}) collective-permute-start(bf16[208,768]{1,0:T(8,128)(2,1)S(1)} %fusion.53), channel_id=1, source_target_pairs={{0,16},{1,17},{2,18},{3,19},{4,20},{5,21},{6,22},{7,23},{8,24},{9,... | collective-permute-start | bytes 958472 | tf_op jit(solution)/shard_map/ppermute | solution.py:232
  185.7 11.0 %copy-start.49 = (bf16[208,768]{1,0:T(8,128)(2,1)}, bf16[208,768]{1,0:T(8,128)(2,1)S(1)}, u32[]{:S(2)}) copy-start(bf16[208,768]{1,0:T(8,128)(2,1)S(1)} %fusion.54) | copy-start | bytes 958468
  185.7 10.8 %collective-permute-start.1 = (bf16[208,768]{1,0:T(8,128)(2,1)S(1)}, bf16[208,768]{1,0:T(8,128)(2,1)S(1)}, u32[]{:S(2)}, u32[]{:S(2)}) collective-permute-start(bf16[208,768]{1,0:T(8,128)(2,1)S(1)} %fusion.54), channel_id=1, source_target_pairs={{0,16},{1,17},{2,18},{3,19},{4,20},{5,21},{6,22},{7,23},{8,24},{9,... | collective-permute-start | bytes 958472 | tf_op jit(solution)/shard_map/ppermute | solution.py:232
  205.9 10.1 %copy-start.51 = (bf16[208,768]{1,0:T(8,128)(2,1)}, bf16[208,768]{1,0:T(8,128)(2,1)S(1)}, u32[]{:S(2)}) copy-start(bf16[208,768]{1,0:T(8,128)(2,1)S(1)} %fusion.55) | copy-start | bytes 958468
  205.9 9.9 %collective-permute-start.2 = (bf16[208,768]{1,0:T(8,128)(2,1)S(1)}, bf16[208,768]{1,0:T(8,128)(2,1)S(1)}, u32[]{:S(2)}, u32[]{:S(2)}) collective-permute-start(bf16[208,768]{1,0:T(8,128)(2,1)S(1)} %fusion.55), channel_id=1, source_target_pairs={{0,16},{1,17},{2,18},{3,19},{4,20},{5,21},{6,22},{7,23},{8,24},{9,... | collective-permute-start | bytes 958472 | tf_op jit(solution)/shard_map/ppermute | solution.py:232
  224.7 10.4 %copy-start.53 = (bf16[208,768]{1,0:T(8,128)(2,1)}, bf16[208,768]{1,0:T(8,128)(2,1)S(1)}, u32[]{:S(2)}) copy-start(bf16[208,768]{1,0:T(8,128)(2,1)S(1)} %fusion.56) | copy-start | bytes 958468
  224.7 8.9 %collective-permute-start.3 = (bf16[208,768]{1,0:T(8,128)(2,1)S(1)}, bf16[208,768]{1,0:T(8,128)(2,1)S(1)}, u32[]{:S(2)}, u32[]{:S(2)}) collective-permute-start(bf16[208,768]{1,0:T(8,128)(2,1)S(1)} %fusion.56), channel_id=1, source_target_pairs={{0,16},{1,17},{2,18},{3,19},{4,20},{5,21},{6,22},{7,23},{8,24},{9,... | collective-permute-start | bytes 958472 | tf_op jit(solution)/shard_map/ppermute | solution.py:232
  229.3 5.8 %copy-start.59 = (bf16[1040,768]{1,0:T(8,128)(2,1)}, bf16[1040,768]{1,0:T(8,128)(2,1)S(1)}, u32[]{:S(2)}) copy-start(bf16[1040,768]{1,0:T(8,128)(2,1)S(1)} %constant_dynamic-update-slice_fusion.30) | copy-start | bytes 4792324
  237.3 7.0 %copy-start.11 = (f32[208,768]{1,0:T(8,128)}, f32[208,768]{1,0:T(8,128)S(1)}, u32[]{:S(2)}) copy-start(f32[208,768]{1,0:T(8,128)S(1)} %get-tuple-element.210) | copy-start | bytes 1916932
  240.8 75.5 %copy-start.25 = (bf16[208,3072]{1,0:T(8,128)(2,1)}, bf16[208,3072]{1,0:T(8,128)(2,1)S(1)}, u32[]{:S(2)}) copy-start(bf16[208,3072]{1,0:T(8,128)(2,1)S(1)} %get-tuple-element.28) | copy-start | bytes 3833860
  245.4 6.9 %copy-start.7 = (f32[208,768]{1,0:T(8,128)}, f32[208,768]{1,0:T(8,128)S(1)}, u32[]{:S(2)}) copy-start(f32[208,768]{1,0:T(8,128)S(1)} %get-tuple-element.105) | copy-start | bytes 1916932
  252.7 10.9 %copy-start.33 = (bf16[208,768]{1,0:T(8,128)(2,1)}, bf16[208,768]{1,0:T(8,128)(2,1)S(1)}, u32[]{:S(2)}) copy-start(bf16[208,768]{1,0:T(8,128)(2,1)S(1)} %fusion.90) | copy-start | bytes 958468
  252.7 9.2 %copy-start.73 = (bf16[208,3072]{1,0:T(8,128)(2,1)S(1)}, bf16[208,3072]{1,0:T(8,128)(2,1)}, u32[]{:S(2)}) copy-start(bf16[208,3072]{1,0:T(8,128)(2,1)} %get-tuple-element.30) | copy-start | bytes 3833860
  252.7 9.0 %collective-permute-start.4 = (bf16[208,768]{1,0:T(8,128)(2,1)S(1)}, bf16[208,768]{1,0:T(8,128)(2,1)S(1)}, u32[]{:S(2)}, u32[]{:S(2)}) collective-permute-start(bf16[208,768]{1,0:T(8,128)(2,1)S(1)} %fusion.90), channel_id=1, source_target_pairs={{16,0},{17,1},{18,2},{19,3},{20,4},{21,5},{22,6},{23,7},{24,8},{25... | collective-permute-start | bytes 958472 | tf_op jit(solution)/shard_map/ppermute | solution.py:250
  265.8 6.9 %copy-start.8 = (f32[208,768]{1,0:T(8,128)}, f32[208,768]{1,0:T(8,128)S(1)}, u32[]{:S(2)}) copy-start(f32[208,768]{1,0:T(8,128)S(1)} %get-tuple-element.103) | copy-start | bytes 1916932
  273.0 9.2 %copy-start.35 = (bf16[208,768]{1,0:T(8,128)(2,1)}, bf16[208,768]{1,0:T(8,128)(2,1)S(1)}, u32[]{:S(2)}) copy-start(bf16[208,768]{1,0:T(8,128)(2,1)S(1)} %fusion.99) | copy-start | bytes 958468
  273.0 9.2 %copy-start.72 = (bf16[208,3072]{1,0:T(8,128)(2,1)S(1)}, bf16[208,3072]{1,0:T(8,128)(2,1)}, u32[]{:S(2)}) copy-start(bf16[208,3072]{1,0:T(8,128)(2,1)} %get-tuple-element.31) | copy-start | bytes 3833860
  273.0 9.0 %collective-permute-start.5 = (bf16[208,768]{1,0:T(8,128)(2,1)S(1)}, bf16[208,768]{1,0:T(8,128)(2,1)S(1)}, u32[]{:S(2)}, u32[]{:S(2)}) collective-permute-start(bf16[208,768]{1,0:T(8,128)(2,1)S(1)} %fusion.99), channel_id=1, source_target_pairs={{16,0},{17,1},{18,2},{19,3},{20,4},{21,5},{22,6},{23,7},{24,8},{25... | collective-permute-start | bytes 958472 | tf_op jit(solution)/shard_map/ppermute | solution.py:250
  286.1 6.9 %copy-start.9 = (f32[208,768]{1,0:T(8,128)}, f32[208,768]{1,0:T(8,128)S(1)}, u32[]{:S(2)}) copy-start(f32[208,768]{1,0:T(8,128)S(1)} %get-tuple-element.101) | copy-start | bytes 1916932
  293.4 10.9 %copy-start.37 = (bf16[208,768]{1,0:T(8,128)(2,1)}, bf16[208,768]{1,0:T(8,128)(2,1)S(1)}, u32[]{:S(2)}) copy-start(bf16[208,768]{1,0:T(8,128)(2,1)S(1)} %fusion.108) | copy-start | bytes 958468
  293.4 9.2 %copy-start.71 = (bf16[208,3072]{1,0:T(8,128)(2,1)S(1)}, bf16[208,3072]{1,0:T(8,128)(2,1)}, u32[]{:S(2)}) copy-start(bf16[208,3072]{1,0:T(8,128)(2,1)} %get-tuple-element.32) | copy-start | bytes 3833860
  293.4 9.0 %collective-permute-start.6 = (bf16[208,768]{1,0:T(8,128)(2,1)S(1)}, bf16[208,768]{1,0:T(8,128)(2,1)S(1)}, u32[]{:S(2)}, u32[]{:S(2)}) collective-permute-start(bf16[208,768]{1,0:T(8,128)(2,1)S(1)} %fusion.108), channel_id=1, source_target_pairs={{16,0},{17,1},{18,2},{19,3},{20,4},{21,5},{22,6},{23,7},{24,8},{25... | collective-permute-start | bytes 958472 | tf_op jit(solution)/shard_map/ppermute | solution.py:250
  295.3 8.9 %copy-start.56 = (bf16[1040,768]{1,0:T(8,128)(2,1)}, bf16[1040,768]{1,0:T(8,128)(2,1)S(1)}, u32[]{:S(2)}) copy-start(bf16[1040,768]{1,0:T(8,128)(2,1)S(1)} %constant_dynamic-update-slice_fusion.19) | copy-start | bytes 4792324
  295.6 8.7 %copy-start.55 = (bf16[1040,768]{1,0:T(8,128)(2,1)}, bf16[1040,768]{1,0:T(8,128)(2,1)S(1)}, u32[]{:S(2)}) copy-start(bf16[1040,768]{1,0:T(8,128)(2,1)S(1)} %constant_dynamic-update-slice_fusion.9) | copy-start | bytes 4792324
  306.5 7.9 %copy-start.10 = (f32[208,768]{1,0:T(8,128)}, f32[208,768]{1,0:T(8,128)S(1)}, u32[]{:S(2)}) copy-start(f32[208,768]{1,0:T(8,128)S(1)} %get-tuple-element.97) | copy-start | bytes 1916932
  314.7 9.2 %copy-start.39 = (bf16[208,768]{1,0:T(8,128)(2,1)}, bf16[208,768]{1,0:T(8,128)(2,1)S(1)}, u32[]{:S(2)}) copy-start(bf16[208,768]{1,0:T(8,128)(2,1)S(1)} %fusion.117) | copy-start | bytes 958468
  314.7 9.2 %copy-start.70 = (bf16[208,3072]{1,0:T(8,128)(2,1)S(1)}, bf16[208,3072]{1,0:T(8,128)(2,1)}, u32[]{:S(2)}) copy-start(bf16[208,3072]{1,0:T(8,128)(2,1)} %get-tuple-element.33) | copy-start | bytes 3833860
  314.7 9.0 %collective-permute-start.7 = (bf16[208,768]{1,0:T(8,128)(2,1)S(1)}, bf16[208,768]{1,0:T(8,128)(2,1)S(1)}, u32[]{:S(2)}, u32[]{:S(2)}) collective-permute-start(bf16[208,768]{1,0:T(8,128)(2,1)S(1)} %fusion.117), channel_id=1, source_target_pairs={{16,0},{17,1},{18,2},{19,3},{20,4},{21,5},{22,6},{23,7},{24,8},{25... | collective-permute-start | bytes 958472 | tf_op jit(solution)/shard_map/ppermute | solution.py:250
  329.3 5.6 copy-start.4
  343.6 7.7 %copy-start.24 = (bf16[208,768]{1,0:T(8,128)(2,1)S(1)}, bf16[208,768]{1,0:T(8,128)(2,1)}, u32[]{:S(2)}) copy-start(bf16[208,768]{1,0:T(8,128)(2,1)} %copy-done.23) | copy-start | bytes 958468
  343.6 7.7 %copy-start.60 = (bf16[1040,768]{1,0:T(8,128)(2,1)S(1)}, bf16[1040,768]{1,0:T(8,128)(2,1)}, u32[]{:S(2)}) copy-start(bf16[1040,768]{1,0:T(8,128)(2,1)} %get-tuple-element.180) | copy-start | bytes 4792324
  345.6 5.8 %copy-start.22 = (bf16[208,768]{1,0:T(8,128)(2,1)S(1)}, bf16[208,768]{1,0:T(8,128)(2,1)}, u32[]{:S(2)}) copy-start(bf16[208,768]{1,0:T(8,128)(2,1)} %copy-done.21) | copy-start | bytes 958468
  412.0 4.3 copy-start.50
  412.0 4.3 copy-start.52
  412.0 4.3 copy-start.54
  412.0 4.3 copy-start.64
  (40 other events, 90.5 us)
Sparse Core Ops, SparseCore 0:
  21.9 115.7 all-gather.2
  410.9 146.1 reduce-scatter.1
